TPU v7x, 32 devices: a whole 2x2x4 slice. The times are simulated.
32 devices in a mesh: dp: 2 (over x), seq: 4 (over z), fsdp: 4 (over y, core).
Axes of the slice: x: 2, y: 2, z: 4, core: 2. Of those that a mesh axis runs over, the one named last changes fastest.
Arguments:
- tokens: bfloat16 [2, 8, 2048, 768], P(None, ('dp', 'fsdp'), 'seq'), may hold values from -6 to 6
- lengths: int32 [2, 8], replicated, may hold values from 1 to 2048, as said below
- in_weight: bfloat16 [768, 2304], P(('dp', 'seq'), 'fsdp'), may hold values from -0.21875 to 0.21875
- in_bias: bfloat16 [1536], P(('dp', 'seq')), may hold values from -3 to 3
- out_weight: bfloat16 [768, 768], P(('dp', 'seq'), 'fsdp'), may hold values from -6 to 6
- out_bias: bfloat16 [768], P(('dp', 'seq')), may hold values from -3 to 3
- mid_gain: bfloat16 [768], P(('dp', 'seq')), may hold values from 0.099609375 to 1.8984375
- mid_shift: bfloat16 [768], P(('dp', 'seq')), may hold values from -3 to 3
- up_weight: bfloat16 [768, 3072], P(('dp', 'seq'), 'fsdp'), may hold values from -0.21875 to 0.21875
- up_bias: bfloat16 [3072], P(('dp', 'seq')), may hold values from -3 to 3
- down_weight: bfloat16 [3072, 768], P(('dp', 'seq'), 'fsdp'), may hold values from -0.109375 to 0.109375
- down_bias: bfloat16 [768], P(('dp', 'seq')), may hold values from -3 to 3
- last_gain: bfloat16 [768], P(('dp', 'seq')), may hold values from 0.099609375 to 1.8984375
- last_shift: bfloat16 [768], P(('dp', 'seq')), may hold values from -3 to 3
- grad_output: bfloat16 [2, 8, 2048, 768], P(None, ('dp', 'fsdp'), 'seq'), may hold values from -6 to 6
Outputs:
- output: bfloat16 [2, 8, 2048, 768], P(None, ('dp', 'fsdp'), 'seq')
- grad_tokens: float32 [2, 8, 2048, 768], P(None, ('dp', 'fsdp'), 'seq')
- grad_in_weight: float32 [768, 2304], P(('dp', 'seq'), 'fsdp')
- grad_in_bias: float32 [1536], P(('dp', 'seq'))
- grad_out_weight: float32 [768, 768], P(('dp', 'seq'), 'fsdp')
- grad_out_bias: float32 [768], P(('dp', 'seq'))
- grad_mid_gain: float32 [768], P(('dp', 'seq'))
- grad_mid_shift: float32 [768], P(('dp', 'seq'))
- grad_up_weight: float32 [768, 3072], P(('dp', 'seq'), 'fsdp')
- grad_up_bias: float32 [3072], P(('dp', 'seq'))
- grad_down_weight: float32 [3072, 768], P(('dp', 'seq'), 'fsdp')
- grad_down_bias: float32 [768], P(('dp', 'seq'))
- grad_last_gain: float32 [768], P(('dp', 'seq'))
- grad_last_shift: float32 [768], P(('dp', 'seq'))
Inputs may be any that keep to these rules, and one draw needn't show every extreme that they name: lengths[m, b] counts the valid tokens of sequence b of micro-batch m, the first ones; the rest is padding. Of the 2 sequences b = j * 1 to (j + 1) - 1 of all micro-batches, at least one has length 2048.
All inputs are finite; a program needn't handle non-finite values.
Results may differ from a plain program's by a relative error of at most 0.02.
Values may be sent and summed in bfloat16 or wider, within the bound.
No kernel may reach another device: no remote copies, remote signals or barrier semaphores. Data moves between devices by JAX's collectives and lax.ppermute only.
A program may use at most 384 MiB of HBM per device.

v0:
```python
import math

import jax
import jax.numpy as jnp
from jax import lax
from jax.sharding import PartitionSpec as P

D = 768
HEADS = 12
HEAD = 64
FF = 3072
MICRO = 2


epsilon = 1e-05


def standardize(hidden):
    centered = hidden - jnp.mean(hidden, axis=-1, keepdims=True)
    scale = lax.rsqrt(jnp.mean(centered * centered, axis=-1, keepdims=True) + epsilon)
    return (centered * scale, scale)


def norm_back(grad_out, standard, scale, gain):
    spread = grad_out * gain
    return scale * (
        spread
        - jnp.mean(spread, axis=-1, keepdims=True)
        - standard * jnp.mean(spread * standard, axis=-1, keepdims=True)
    )


def gelu_slope(value):
    return 0.5 * (1.0 + lax.erf(value * (1.0 / math.sqrt(2.0)))) + value * jnp.exp(
        -0.5 * value * value
    ) * (1.0 / math.sqrt(2.0 * math.pi))


def with_key_zeros(query_value):
    paired = query_value.astype(jnp.float32).reshape(HEADS, 2, HEAD)
    return jnp.stack([paired[:, 0], jnp.zeros_like(paired[:, 0]), paired[:, 1]], axis=1).reshape(
        3 * D
    )


def gather_weights(in_weight, out_weight, up_weight, down_weight, vectors):
    columns = (
        lax.all_gather(in_weight, "fsdp", axis=1, tiled=True),
        lax.all_gather(out_weight, "fsdp", axis=1, tiled=True),
        lax.all_gather(up_weight, "fsdp", axis=1, tiled=True),
        lax.all_gather(down_weight, "fsdp", axis=1, tiled=True),
    )
    return (
        lax.all_gather(columns[0], ("dp", "seq"), axis=0, tiled=True),
        lax.all_gather(columns[1], ("dp", "seq"), axis=0, tiled=True),
        lax.all_gather(columns[2], ("dp", "seq"), axis=0, tiled=True),
        lax.all_gather(columns[3], ("dp", "seq"), axis=0, tiled=True),
        lax.all_gather(vectors[0], ("dp", "seq"), axis=0, tiled=True),
        lax.all_gather(vectors[1], ("dp", "seq"), axis=0, tiled=True),
        lax.all_gather(vectors[2], ("dp", "seq"), axis=0, tiled=True),
        lax.all_gather(vectors[3], ("dp", "seq"), axis=0, tiled=True),
        lax.all_gather(vectors[4], ("dp", "seq"), axis=0, tiled=True),
        lax.all_gather(vectors[5], ("dp", "seq"), axis=0, tiled=True),
        lax.all_gather(vectors[6], ("dp", "seq"), axis=0, tiled=True),
        lax.all_gather(vectors[7], ("dp", "seq"), axis=0, tiled=True),
    )


def reduce_rows(matrices, vectors):
    summed = (
        lax.psum_scatter(matrices[0], ("dp", "seq"), scatter_dimension=0, tiled=True),
        lax.psum_scatter(matrices[1], ("dp", "seq"), scatter_dimension=0, tiled=True),
        lax.psum_scatter(matrices[2], ("dp", "seq"), scatter_dimension=0, tiled=True),
        lax.psum_scatter(matrices[3], ("dp", "seq"), scatter_dimension=0, tiled=True),
        lax.psum_scatter(vectors[0], ("dp", "seq"), scatter_dimension=0, tiled=True),
        lax.psum_scatter(vectors[1], ("dp", "seq"), scatter_dimension=0, tiled=True),
        lax.psum_scatter(vectors[2], ("dp", "seq"), scatter_dimension=0, tiled=True),
        lax.psum_scatter(vectors[3], ("dp", "seq"), scatter_dimension=0, tiled=True),
        lax.psum_scatter(vectors[4], ("dp", "seq"), scatter_dimension=0, tiled=True),
        lax.psum_scatter(vectors[5], ("dp", "seq"), scatter_dimension=0, tiled=True),
        lax.psum_scatter(vectors[6], ("dp", "seq"), scatter_dimension=0, tiled=True),
        lax.psum_scatter(vectors[7], ("dp", "seq"), scatter_dimension=0, tiled=True),
    )
    return (summed[:4], summed[4:])


def reduce_cols(matrices, vectors):
    summed = (
        lax.psum_scatter(
            matrices[0].astype(jnp.bfloat16), "fsdp", scatter_dimension=1, tiled=True
        ).astype(jnp.float32),
        lax.psum_scatter(
            matrices[1].astype(jnp.bfloat16), "fsdp", scatter_dimension=1, tiled=True
        ).astype(jnp.float32),
        lax.psum_scatter(
            matrices[2].astype(jnp.bfloat16), "fsdp", scatter_dimension=1, tiled=True
        ).astype(jnp.float32),
        lax.psum_scatter(
            matrices[3].astype(jnp.bfloat16), "fsdp", scatter_dimension=1, tiled=True
        ).astype(jnp.float32),
    )
    totals = lax.psum(
        (
            vectors[0],
            vectors[1],
            vectors[2],
            vectors[3],
            vectors[4],
            vectors[5],
            vectors[6],
            vectors[7],
        ),
        "fsdp",
    )
    return (tuple(summed), tuple(totals))


def row_sum(values):
    return jnp.sum(values.astype(jnp.float32), axis=0)


def local(
    tokens,
    lengths,
    in_weight,
    in_bias,
    out_weight,
    out_bias,
    mid_gain,
    mid_shift,
    up_weight,
    up_bias,
    down_weight,
    down_bias,
    last_gain,
    last_shift,
    grad_output,
):
    seqs_local = tokens.shape[1]
    rows = tokens.shape[2]
    group_index = lax.axis_index("dp") * lax.axis_size("fsdp") + lax.axis_index("fsdp")
    factor = 1.0 / math.sqrt(HEAD)
    vectors = (in_bias, out_bias, mid_gain, mid_shift, up_bias, down_bias, last_gain, last_shift)
    acc_in = jnp.zeros((D, 3 * D), jnp.float32)
    acc_out = jnp.zeros((D, D), jnp.float32)
    acc_up = jnp.zeros((D, FF), jnp.float32)
    acc_down = jnp.zeros((FF, D), jnp.float32)
    vec_in = jnp.zeros((2 * D,), jnp.float32)
    vec_out = jnp.zeros((D,), jnp.float32)
    vec_mid_gain = jnp.zeros((D,), jnp.float32)
    vec_mid_shift = jnp.zeros((D,), jnp.float32)
    vec_up = jnp.zeros((FF,), jnp.float32)
    vec_down = jnp.zeros((D,), jnp.float32)
    vec_last_gain = jnp.zeros((D,), jnp.float32)
    vec_last_shift = jnp.zeros((D,), jnp.float32)
    results = []
    grad_inputs = []
    for micro in range(MICRO):
        weights = gather_weights(in_weight, out_weight, up_weight, down_weight, vectors)
        (
            in_matrix,
            out_matrix,
            up_matrix,
            down_matrix,
            in_vector,
            out_vector,
            mid_scale,
            mid_offset,
            up_vector,
            down_vector,
            last_scale,
            last_offset,
        ) = weights
        seq_lens = lax.dynamic_slice_in_dim(lengths[micro], group_index * seqs_local, seqs_local)
        flat = tokens[micro].reshape(-1, D)
        proj = jnp.dot(flat, in_matrix, preferred_element_type=jnp.float32) + with_key_zeros(
            in_vector
        )
        split = proj.astype(jnp.bfloat16).reshape(seqs_local, rows, HEADS, 3, HEAD)
        queries = split[:, :, :, 0]
        keys = split[:, :, :, 1].reshape(seqs_local, rows, D)
        values = split[:, :, :, 2].reshape(seqs_local, rows, D)
        peak_old = jnp.full((seqs_local, rows, HEADS), -1e30, jnp.float32)
        key_piece = lax.all_gather(keys, "seq", axis=1, tiled=True)
        value_piece = lax.all_gather(values, "seq", axis=1, tiled=True)
        count = key_piece.shape[1]
        key_piece = key_piece.reshape(seqs_local, count, HEADS, HEAD)
        value_piece = value_piece.reshape(seqs_local, count, HEADS, HEAD)
        scores = (
            jnp.einsum("sqhd,skhd->sqhk", queries, key_piece, preferred_element_type=jnp.float32)
            * factor
        )
        valid = jnp.arange(count, dtype=jnp.int32)[None, :] < seq_lens[:, None]
        scores = jnp.where(valid[:, None, None, :], scores, -jnp.inf)
        peak = jnp.maximum(peak_old, jnp.max(scores, axis=-1))
        weights_now = jnp.exp(scores - peak[..., None])
        total = jnp.sum(weights_now, axis=-1)
        summed = jnp.einsum(
            "sqhk,skhd->sqhd",
            weights_now.astype(jnp.bfloat16),
            value_piece,
            preferred_element_type=jnp.float32,
        )
        peak, total, summed = (peak, total, summed)
        attended = summed / total[..., None]
        log_total = peak + jnp.log(total)
        back_tokens = attended.astype(jnp.bfloat16).reshape(-1, D)
        mixed = jnp.dot(
            back_tokens, out_matrix, preferred_element_type=jnp.float32
        ) + out_vector.astype(jnp.float32)
        first_std, first_scale = standardize(flat.astype(jnp.float32) + mixed)
        normed = first_std * mid_scale.astype(jnp.float32) + mid_offset.astype(jnp.float32)
        normed_low = normed.astype(jnp.bfloat16)
        pre_up = jnp.dot(
            normed_low, up_matrix, preferred_element_type=jnp.float32
        ) + up_vector.astype(jnp.float32)
        act_low = jax.nn.gelu(pre_up, approximate=False).astype(jnp.bfloat16)
        branch = jnp.dot(
            act_low, down_matrix, preferred_element_type=jnp.float32
        ) + down_vector.astype(jnp.float32)
        second_std, second_scale = standardize(normed + branch)
        result = second_std * last_scale.astype(jnp.float32) + last_offset.astype(jnp.float32)
        results.append(result.astype(jnp.bfloat16).reshape(seqs_local, rows, D))
        back_weights = gather_weights(in_weight, out_weight, up_weight, down_weight, vectors)
        in_matrix, out_matrix, up_matrix, down_matrix = (
            back_weights[0],
            back_weights[1],
            back_weights[2],
            back_weights[3],
        )
        mid_scale, last_scale = (back_weights[6], back_weights[10])
        grad_top = grad_output[micro].reshape(-1, D).astype(jnp.float32)
        vec_last_gain = vec_last_gain + jnp.sum(grad_top * second_std, axis=0)
        vec_last_shift = vec_last_shift + jnp.sum(grad_top, axis=0)
        grad_second = norm_back(grad_top, second_std, second_scale, last_scale.astype(jnp.float32))
        grad_branch = grad_second.astype(jnp.bfloat16)
        vec_down = vec_down + row_sum(grad_branch)
        acc_down = acc_down + jnp.dot(act_low.T, grad_branch, preferred_element_type=jnp.float32)
        grad_pre = (
            jnp.dot(grad_branch, down_matrix.T, preferred_element_type=jnp.float32)
            * gelu_slope(pre_up)
        ).astype(jnp.bfloat16)
        vec_up = vec_up + row_sum(grad_pre)
        acc_up = acc_up + jnp.dot(normed_low.T, grad_pre, preferred_element_type=jnp.float32)
        grad_normed = grad_second + jnp.dot(
            grad_pre, up_matrix.T, preferred_element_type=jnp.float32
        )
        vec_mid_gain = vec_mid_gain + jnp.sum(grad_normed * first_std, axis=0)
        vec_mid_shift = vec_mid_shift + jnp.sum(grad_normed, axis=0)
        grad_first = norm_back(grad_normed, first_std, first_scale, mid_scale.astype(jnp.float32))
        grad_mixed = grad_first.astype(jnp.bfloat16)
        vec_out = vec_out + row_sum(grad_mixed)
        acc_out = acc_out + jnp.dot(back_tokens.T, grad_mixed, preferred_element_type=jnp.float32)
        grad_attended = jnp.dot(
            grad_mixed, out_matrix.T, preferred_element_type=jnp.float32
        ).astype(jnp.bfloat16)
        grad_heads = grad_attended.reshape(seqs_local, rows, HEADS, HEAD)
        delta = jnp.sum(grad_heads.astype(jnp.float32) * attended, axis=-1)
        attend_key_piece = lax.all_gather(keys, "seq", axis=1, tiled=True)
        attend_value_piece = lax.all_gather(values, "seq", axis=1, tiled=True)
        attend_count = attend_key_piece.shape[1]
        attend_key_piece = attend_key_piece.reshape(seqs_local, attend_count, HEADS, HEAD)
        attend_value_piece = attend_value_piece.reshape(seqs_local, attend_count, HEADS, HEAD)
        attend_valid = jnp.arange(attend_count, dtype=jnp.int32)[None, :] < seq_lens[:, None]
        score_scores = (
            jnp.einsum(
                "sqhd,skhd->sqhk", queries, attend_key_piece, preferred_element_type=jnp.float32
            )
            * factor
        )
        score_scores = jnp.where(attend_valid[:, None, None, :], score_scores, -jnp.inf)
        probs = jnp.exp(score_scores - log_total[..., None])
        grad_probs = jnp.einsum(
            "sqhd,skhd->sqhk", grad_heads, attend_value_piece, preferred_element_type=jnp.float32
        )
        grad_scores = (probs * (grad_probs - delta[..., None])).astype(jnp.bfloat16)
        grad_queries = (
            jnp.einsum(
                "sqhk,skhd->sqhd", grad_scores, attend_key_piece, preferred_element_type=jnp.float32
            )
            * factor
        )
        key_piece_grad = (
            jnp.einsum("sqhk,sqhd->skhd", grad_scores, queries, preferred_element_type=jnp.float32)
            * factor
        )
        value_piece_grad = jnp.einsum(
            "sqhk,sqhd->skhd",
            probs.astype(jnp.bfloat16),
            grad_heads,
            preferred_element_type=jnp.float32,
        )
        key_terms = key_piece_grad.reshape(seqs_local, attend_count, D)
        value_terms = value_piece_grad.reshape(seqs_local, attend_count, D)
        folded = (grad_queries, key_terms, value_terms)
        grad_queries, key_terms, value_terms = folded
        key_sums, value_sums = (
            lax.psum_scatter(
                key_terms.astype(jnp.bfloat16), "seq", scatter_dimension=1, tiled=True
            ).astype(jnp.float32),
            lax.psum_scatter(
                value_terms.astype(jnp.bfloat16), "seq", scatter_dimension=1, tiled=True
            ).astype(jnp.float32),
        )
        grad_stack = jnp.stack(
            [
                grad_queries,
                key_sums.reshape(seqs_local, rows, HEADS, HEAD),
                value_sums.reshape(seqs_local, rows, HEADS, HEAD),
            ],
            axis=3,
        )
        grad_proj = grad_stack.astype(jnp.bfloat16).reshape(-1, 3 * D)
        bias_terms = row_sum(grad_proj).reshape(HEADS, 3, HEAD)
        vec_in = vec_in + jnp.stack([bias_terms[:, 0], bias_terms[:, 2]], axis=1).reshape(2 * D)
        acc_in = acc_in + jnp.dot(flat.T, grad_proj, preferred_element_type=jnp.float32)
        grad_input = grad_first + jnp.dot(
            grad_proj, in_matrix.T, preferred_element_type=jnp.float32
        )
        grad_inputs.append(grad_input.reshape(seqs_local, rows, D))
    matrices = (acc_in, acc_out, acc_up, acc_down)
    vector_grads = (
        vec_in,
        vec_out,
        vec_mid_gain,
        vec_mid_shift,
        vec_up,
        vec_down,
        vec_last_gain,
        vec_last_shift,
    )
    matrices, vector_grads = reduce_rows(matrices, vector_grads)
    matrices, vector_grads = reduce_cols(matrices, vector_grads)
    return (
        jnp.stack(results, axis=0),
        jnp.stack(grad_inputs, axis=0),
        matrices[0],
        vector_grads[0],
        matrices[1],
        vector_grads[1],
        vector_grads[2],
        vector_grads[3],
        matrices[2],
        vector_grads[4],
        matrices[3],
        vector_grads[5],
        vector_grads[6],
        vector_grads[7],
    )


def solution(mesh):
    return jax.shard_map(
        local,
        mesh=mesh,
        in_specs=(
            P(None, ("dp", "fsdp"), "seq", None),
            P(),
            P(("dp", "seq"), "fsdp"),
            P(("dp", "seq")),
            P(("dp", "seq"), "fsdp"),
            P(("dp", "seq")),
            P(("dp", "seq")),
            P(("dp", "seq")),
            P(("dp", "seq"), "fsdp"),
            P(("dp", "seq")),
            P(("dp", "seq"), "fsdp"),
            P(("dp", "seq")),
            P(("dp", "seq")),
            P(("dp", "seq")),
            P(None, ("dp", "fsdp"), "seq", None),
        ),
        out_specs=(
            P(None, ("dp", "fsdp"), "seq", None),
            P(None, ("dp", "fsdp"), "seq", None),
            P(("dp", "seq"), "fsdp"),
            P(("dp", "seq")),
            P(("dp", "seq"), "fsdp"),
            P(("dp", "seq")),
            P(("dp", "seq")),
            P(("dp", "seq")),
            P(("dp", "seq"), "fsdp"),
            P(("dp", "seq")),
            P(("dp", "seq"), "fsdp"),
            P(("dp", "seq")),
            P(("dp", "seq")),
            P(("dp", "seq")),
        ),
        check_vma=False,
    )
```

profile of v0, /device:TPU:0, one launch (start us, length us, event | category | flops | bytes accessed | tf_op | source)
XLA Modules:
  0.0 1481.7 jit_solution(5260380105037760198)
XLA Ops:
  26.1 38.8 %all-reduce.17 = (bf16[1536]{0:T(1024)(128)(2,1)S(1)}, bf16[768]{0:T(1024)(128)(2,1)S(1)}, bf16[768]{0:T(1024)(128)(2,1)S(1)}, bf16[768]{0:T(1024)(128)(2,1)S(1)...) all-reduce(bf16[1536]{0:T(1024)(128)(2,1)S(1)} %dynamic-update-slic, ...), channel_id=1, replica_groups=mesh['dp'=2,'seq'=4,'fsdp'=4] {'dp','seq'}, use_global_device_ids=true, to_apply=%add | all-reduce | flops 6144 | bytes 24576
  65.2 19.3 %all-gather.11.cloned.1.call-done = bf16[768,2304]{1,0:T(8,128)(2,1)} async-done(((bf16[96,2304]{1,0:T(8,128)(2,1)}), bf16[768,2304]{1,0:T(8,128)(2,1)}) %all-gather.11.cloned.1.call-update) | async-done | bytes 3538960 | tf_op jit(solution)/shard_map/all_gather | solution.py:54
  133.4 27.3 %all-gather.1 = bf16[8,1,384]{2,1,0:T(2,128)(2,1)S(1)} all-gather(bf16[1,1,384]{2,1,0:T(2,128)(2,1)S(1)} %reshape.645), channel_id=1, replica_groups=mesh['dp'=2,'seq'=4,'fsdp'=4] {'dp','seq'}, dimensions={0}, use_global_device_ids=true | all-gather | bytes 6912 | tf_op jit(solution)/shard_map/all_gather | solution.py:62
  162.5 20.4 %bitcast_reduce_fusion.1 = (f32[512,12]{0,1:T(8,128)S(1)}, f32[12,2048,512]{2,1,0:T(8,128)}) fusion(pred[2048]{0:T(1024)(128)(4,1)S(1)} %iota_compare_fusion.1, bf16[2048,12,64]{0,2,1:T(8,128)(2,1)} %bitcast.372, bf16[1,512,12,3,64]{1,4,3,2,0:T(8,128)(2,1)S(1)} %bitcast.379), kind=kOutput, calls=%fused_computation.14 | convolution fusion | flops 1648355328 | bytes 54290432 | tf_op jit(solution)/shard_map/sqhd,skhd->sqhk/dot_general | solution.py:190
  182.9 22.1 %fusion.9 = f32[512,12]{0,1:T(8,128)S(1)} fusion(f32[12,2048,512]{2,1,0:T(8,128)} %get-tuple-element.163, f32[512,12]{0,1:T(8,128)S(1)} %broadcast_maximum_fusion.1, pred[2048]{0:T(1024)(128)(4,1)S(1)} %iota_compare_fusion.1), kind=kLoop, calls=%fused_computation.19 | loop fusion | flops 50325504 | bytes 50382848 | tf_op jit(solution)/shard_map/reduce_sum | solution.py:197
  205.0 15.2 %all-gather.13.cloned.1.call-done = bf16[1,2048,768]{1,2,0:T(8,128)(2,1)} async-done(((bf16[1,512,768]{1,2,0:T(8,128)(2,1)}), bf16[1,2048,768]{1,2,0:T(8,128)(2,1)}) %all-gather.13.cloned.1.call-update) | async-done | bytes 3145744 | tf_op jit(solution)/shard_map/all_gather | solution.py:185
  220.2 21.1 %fusion.143 = (bf16[1,512,12,64]{1,3,2,0:T(8,128)(2,1)S(1)}, f32[1,512,12,64]{1,3,2,0:T(8,128)}) fusion(f32[512,12]{0,1:T(8,128)S(1)} %fusion.9, bf16[2048,12,64]{0,2,1:T(8,128)(2,1)} %bitcast.419, f32[12,2048,512]{2,1,0:T(8,128)} %get-tuple-element.163, f32[512,12]{0,1:T(8,128)S(1)} %broadcast_maximum_fusion.1, pred[2048]{0:T(1024)(128)(4,1)S(1)} %iota_compare_fusion.1), kind=kOutput, calls=%fused_computation.243 | convolution fusion | flops 1661730816 | bytes 55887872 | tf_op jit(solution)/shard_map/sqhk,skhd->sqhd/dot_general | solution.py:198
  241.4 21.2 %all-gather.17.cloned.1.call-done = bf16[768,768]{1,0:T(8,128)(2,1)} async-done(((bf16[96,768]{1,0:T(8,128)(2,1)}), bf16[768,768]{1,0:T(8,128)(2,1)}) %all-gather.17.cloned.1.call-update) | async-done | bytes 1179664 | tf_op jit(solution)/shard_map/all_gather | solution.py:55
  265.8 61.0 %all-gather.25.cloned.1.call-done = bf16[1,2048,768]{1,2,0:T(8,128)(2,1)} async-done(((bf16[1,512,768]{1,2,0:T(8,128)(2,1)}), bf16[1,2048,768]{1,2,0:T(8,128)(2,1)}) %all-gather.25.cloned.1.call-update) | async-done | bytes 3145744 | tf_op jit(solution)/shard_map/all_gather | solution.py:184
  326.8 21.0 %bitcast_reduce_fusion = (f32[512,12]{0,1:T(8,128)S(1)}, f32[12,2048,512]{2,1,0:T(8,128)}) fusion(pred[2048]{0:T(1024)(128)(4,1)S(1)} %iota_compare_fusion, bf16[2048,12,64]{0,2,1:T(8,128)(2,1)} %bitcast.374, bf16[1,512,12,3,64]{1,4,3,2,0:T(8,128)(2,1)} %bitcast.382), kind=kOutput, calls=%fused_computation.8 | convolution fusion | flops 1648355328 | bytes 54290432 | tf_op jit(solution)/shard_map/sqhd,skhd->sqhk/dot_general | solution.py:190
  347.8 22.1 %fusion.12 = f32[512,12]{0,1:T(8,128)S(1)} fusion(f32[12,2048,512]{2,1,0:T(8,128)} %get-tuple-element.169, f32[512,12]{0,1:T(8,128)S(1)} %broadcast_maximum_fusion, pred[2048]{0:T(1024)(128)(4,1)S(1)} %iota_compare_fusion), kind=kLoop, calls=%fused_computation.22 | loop fusion | flops 50325504 | bytes 50382848 | tf_op jit(solution)/shard_map/reduce_sum | solution.py:197
  369.9 21.1 %all-gather.23.cloned.1.call-done = bf16[1,2048,768]{1,2,0:T(8,128)(2,1)} async-done(((bf16[1,512,768]{1,2,0:T(8,128)(2,1)}), bf16[1,2048,768]{1,2,0:T(8,128)(2,1)}) %all-gather.23.cloned.1.call-update) | async-done | bytes 3145744 | tf_op jit(solution)/shard_map/all_gather | solution.py:185
  391.0 21.8 %fusion.145 = (bf16[1,512,12,64]{1,3,2,0:T(8,128)(2,1)S(1)}, f32[1,512,12,64]{1,3,2,0:T(8,128)}) fusion(f32[512,12]{0,1:T(8,128)S(1)} %fusion.12, bf16[2048,12,64]{0,2,1:T(8,128)(2,1)} %bitcast.421, f32[12,2048,512]{2,1,0:T(8,128)} %get-tuple-element.169, f32[512,12]{0,1:T(8,128)S(1)} %broadcast_maximum_fusion, pred[2048]{0:T(1024)(128)(4,1)S(1)} %iota_compare_fusion), kind=kOutput, calls=%fused_computation.245 | convolution fusion | flops 1661730816 | bytes 55887872 | tf_op jit(solution)/shard_map/sqhk,skhd->sqhd/dot_general | solution.py:198
  414.1 57.6 %all-gather.19.cloned.1.call-done = bf16[768,3072]{1,0:T(8,128)(2,1)} async-done(((bf16[96,3072]{1,0:T(8,128)(2,1)}), bf16[768,3072]{1,0:T(8,128)(2,1)}) %all-gather.19.cloned.1.call-update) | async-done | bytes 4718608 | tf_op jit(solution)/shard_map/all_gather | solution.py:56
  479.1 31.2 %fusion.34 = (bf16[512,3072]{1,0:T(8,128)(2,1)}, bf16[512,3072]{1,0:T(8,128)(2,1)}, f32[512,3072]{1,0:T(8,128)}) fusion(f32[3072]{0:T(1024)S(1)} %bitcast.414, f32[512,3072]{1,0:T(8,128)S(1)} %fusion.128, bf16[768,3072]{1,0:T(8,128)(2,1)S(1)} %copy-done.61, f32[512,768]{1,0:T(8,128)S(1)} %copy-done.18, f32[768]{0:T(1024)S(1)} %convert_element_type.356, ...), kind=kOutput, calls=%fused_computation.45 | convolution fusion | flops 2625503232 | bytes 25188352 | tf_op jit(solution)/shard_map/dot_general | solution.py:214
  510.3 42.6 %all-gather.21.cloned.1.call-done = bf16[3072,768]{0,1:T(8,128)(2,1)} async-done(((bf16[384,768]{0,1:T(8,128)(2,1)}), bf16[3072,768]{0,1:T(8,128)(2,1)}) %all-gather.21.cloned.1.call-update) | async-done | bytes 4718608 | tf_op jit(solution)/shard_map/all_gather | solution.py:57
  606.9 31.0 %fusion.18 = bf16[512,12,2048]{0,2,1:T(8,128)(2,1)} fusion(f32[12,2048,512]{2,1,0:T(8,128)} %get-tuple-element.163, f32[512,12]{0,1:T(8,128)S(1)} %multiply_reduce_fusion.4, f32[512,12]{0,1:T(8,128)S(1)} %log_add_fusion.1, pred[2048]{0:T(1024)(128)(4,1)S(1)} %copy-done.44, bf16[2048,12,64]{0,2,1:T(8,128)(2,1)} %bitcast.420, bf16[512,12,64]{0,2,1:T(8,128)(2,1)} %bitcast.408), kind=kOutput, calls=%fused_computation.28 | convolution fusion | flops 1686110208 | bytes 79480832 | tf_op jit(solution)/shard_map/sqhd,skhd->sqhk/dot_general | solution.py:273
  637.9 13.9 multiply_convert_fusion.1
  651.9 21.0 %fusion.69 = bf16[12,64,2048]{2,1,0:T(8,128)(2,1)} fusion(bf16[512,12,64]{0,2,1:T(8,128)(2,1)} %bitcast.409, f32[12,2048,512]{2,1,0:T(8,128)} %get-tuple-element.163, f32[512,12]{0,1:T(8,128)S(1)} %log_add_fusion.1, pred[2048]{0:T(1024)(128)(4,1)S(1)} %copy-done.44), kind=kOutput, calls=%fused_computation.106 | convolution fusion | flops 1662517248 | bytes 54290432 | tf_op jit(solution)/shard_map/sqhk,sqhd->skhd/dot_general | solution.py:287
  683.7 31.3 %fusion.19 = bf16[512,12,2048]{0,2,1:T(8,128)(2,1)} fusion(f32[12,2048,512]{2,1,0:T(8,128)} %get-tuple-element.169, f32[512,12]{0,1:T(8,128)S(1)} %multiply_reduce_fusion.2, f32[512,12]{0,1:T(8,128)S(1)} %log_add_fusion, pred[2048]{0:T(1024)(128)(4,1)S(1)} %copy-done.42, bf16[2048,12,64]{0,2,1:T(8,128)(2,1)} %bitcast.422, bf16[512,12,64]{0,2,1:T(8,128)(2,1)} %bitcast.406), kind=kOutput, calls=%fused_computation.29 | convolution fusion | flops 1686110208 | bytes 79480832 | tf_op jit(solution)/shard_map/sqhd,skhd->sqhk/dot_general | solution.py:273
  715.0 13.9 multiply_convert_fusion
  728.9 21.4 %fusion.66 = bf16[12,64,2048]{2,1,0:T(8,128)(2,1)} fusion(bf16[512,12,64]{0,2,1:T(8,128)(2,1)} %bitcast.407, f32[12,2048,512]{2,1,0:T(8,128)} %get-tuple-element.169, f32[512,12]{0,1:T(8,128)S(1)} %log_add_fusion, pred[2048]{0:T(1024)(128)(4,1)S(1)} %copy-done.42), kind=kOutput, calls=%fused_computation.105 | convolution fusion | flops 1662517248 | bytes 54290432 | tf_op jit(solution)/shard_map/sqhk,sqhd->skhd/dot_general | solution.py:287
  775.4 11.6 multiply_bitcast_fusion.1
  786.9 10.6 multiply_bitcast_fusion
  808.4 41.7 %reduce-scatter.23.cloned.1.call-done = bf16[1,512,768]{1,2,0:T(8,128)(2,1)} async-done(((bf16[1,2048,768]{1,2,0:T(8,128)(2,1)}), bf16[1,512,768]{1,2,0:T(8,128)(2,1)}) %reduce-scatter.23.cloned.1.call-update) | async-done | bytes 786448 | tf_op jit(solution)/shard_map/reduce_scatter | solution.py:298
  850.1 62.6 %reduce-scatter.25.cloned.1.call-done = bf16[1,512,768]{1,2,0:T(8,128)(2,1)} async-done(((bf16[1,2048,768]{1,2,0:T(8,128)(2,1)}), bf16[1,512,768]{1,2,0:T(8,128)(2,1)}) %reduce-scatter.25.cloned.1.call-update) | async-done | bytes 786448 | tf_op jit(solution)/shard_map/reduce_scatter | solution.py:301
  930.1 149.4 %reduce-scatter.35.cloned.1.call-done = f32[384,768]{1,0:T(8,128)} async-done(((f32[3072,768]{1,0:T(8,128)}), f32[384,768]{1,0:T(8,128)}) %reduce-scatter.35.cloned.1.call-update) | async-done | bytes 1179664 | tf_op jit(solution)/shard_map/reduce_scatter | solution.py:74
  1087.7 157.7 %reduce-scatter.31.cloned.1.call-done = f32[96,3072]{1,0:T(8,128)} async-done(((f32[768,3072]{1,0:T(8,128)}), f32[96,3072]{1,0:T(8,128)}) %reduce-scatter.31.cloned.1.call-update) | async-done | bytes 1179664 | tf_op jit(solution)/shard_map/reduce_scatter | solution.py:73
  1250.0 17.0 %reduce-scatter.39.cloned.1.call-done = bf16[192,96]{1,0:T(8,128)(2,1)} async-done(((bf16[768,96]{1,0:T(8,128)(2,1)}), bf16[192,96]{1,0:T(8,128)(2,1)}) %reduce-scatter.39.cloned.1.call-update) | async-done | bytes 36880
  1275.0 124.6 %reduce-scatter.37.cloned.1.call-done = f32[96,2304]{1,0:T(8,128)} async-done(((f32[768,2304]{1,0:T(8,128)}), f32[96,2304]{1,0:T(8,128)}) %reduce-scatter.37.cloned.1.call-update) | async-done | bytes 884752
  1402.0 36.1 %all-reduce.15 = (f32[1536]{0:T(1024)S(1)}, f32[768]{0:T(1024)S(1)}, f32[768]{0:T(1024)S(1)}, f32[768]{0:T(1024)S(1)}, f32[3072]{0:T(1024)S(1)}, /*index=5*/f32[...) all-reduce(f32[1536]{0:T(1024)S(1)} %add.319, ...), channel_id=8, replica_groups=mesh['dp'=2,'seq'=4,'fsdp'=4] {'dp','seq'}, use_global_device_ids=true, to_apply=%region_30.31.clone | all-reduce | flops 9216 | bytes 73728
  1455.4 17.3 %reduce-scatter.27.cloned.1.call-done = bf16[96,576]{0,1:T(8,128)(2,1)} async-done(((bf16[96,2304]{0,1:T(8,128)(2,1)}), bf16[96,576]{0,1:T(8,128)(2,1)}) %reduce-scatter.27.cloned.1.call-update) | async-done | bytes 110608 | tf_op jit(solution)/shard_map/reduce_scatter | solution.py:89
  (324 shorter events, 238.0 us)
Async XLA Ops:
  7.2 77.2 %all-gather.11.cloned.1.call-start = ((), (), s32[]{:S(2)}) async-start(), calls=%async_computation.12 | async-start | bytes 3981312 | tf_op jit(solution)/shard_map/all_gather | solution.py:54
  17.5 145.0 %all-gather.15.cloned.1.call-start = ((), (), s32[]{:S(2)}) async-start(), calls=%async_computation.14 | async-start | bytes 3932160 | tf_op jit(solution)/shard_map/all_gather | solution.py:184
  94.1 126.1 %all-gather.13.cloned.1.call-start = ((), (), s32[]{:S(2)}) async-start(), calls=%async_computation.13 | async-start | bytes 3932160 | tf_op jit(solution)/shard_map/all_gather | solution.py:185
  94.9 167.7 %all-gather.17.cloned.1.call-start = ((), (), s32[]{:S(2)}) async-start(), calls=%async_computation.15 | async-start | bytes 1327104 | tf_op jit(solution)/shard_map/all_gather | solution.py:55
  101.5 225.3 %all-gather.25.cloned.1.call-start = ((), (), s32[]{:S(2)}) async-start(), calls=%async_computation.19 | async-start | bytes 3932160 | tf_op jit(solution)/shard_map/all_gather | solution.py:184
  114.4 276.6 %all-gather.23.cloned.1.call-start = ((), (), s32[]{:S(2)}) async-start(), calls=%async_computation.18 | async-start | bytes 3932160 | tf_op jit(solution)/shard_map/all_gather | solution.py:185
  115.0 356.7 %all-gather.19.cloned.1.call-start = ((), (), s32[]{:S(2)}) async-start(), calls=%async_computation.16 | async-start | bytes 5308416 | tf_op jit(solution)/shard_map/all_gather | solution.py:56
  123.1 429.7 %all-gather.21.cloned.1.call-start = ((), (), s32[]{:S(2)}) async-start(), calls=%async_computation.17 | async-start | bytes 5308416 | tf_op jit(solution)/shard_map/all_gather | solution.py:57
  131.3 666.3 %reduce-scatter.29.cloned.1.call-start = ((), (), s32[]{:S(2)}) async-start(), calls=%async_computation.25 | async-start | bytes 2654208 | tf_op jit(solution)/shard_map/reduce_scatter | solution.py:72
  133.3 257.6 %copy-start.41 = (pred[2048]{0:T(1024)(128)(4,1)}, pred[2048]{0:T(1024)(128)(4,1)S(1)}, u32[]{:S(2)}) copy-start(pred[2048]{0:T(1024)(128)(4,1)S(1)} %iota_compare_fusion) | copy-start | bytes 6148
  133.4 426.1 %copy-start.37 = (f32[768]{0:T(1024)}, f32[768]{0:T(1024)S(1)}, u32[]{:S(2)}) copy-start(f32[768]{0:T(1024)S(1)} %convert_element_type.356) | copy-start | bytes 9220
  596.1 203.6 %reduce-scatter.19.cloned.1.call-start = ((), (), s32[]{:S(2)}) async-start(), calls=%async_computation.20 | async-start | bytes 3932160 | tf_op jit(solution)/shard_map/reduce_scatter | solution.py:298
  651.8 147.9 %reduce-scatter.21.cloned.1.call-start = ((), (), s32[]{:S(2)}) async-start(), calls=%async_computation.21 | async-start | bytes 3932160 | tf_op jit(solution)/shard_map/reduce_scatter | solution.py:301
  672.9 177.2 %reduce-scatter.23.cloned.1.call-start = ((), (), s32[]{:S(2)}) async-start(), calls=%async_computation.22 | async-start | bytes 3932160 | tf_op jit(solution)/shard_map/reduce_scatter | solution.py:298
  728.9 183.8 %reduce-scatter.25.cloned.1.call-start = ((), (), s32[]{:S(2)}) async-start(), calls=%async_computation.23 | async-start | bytes 3932160 | tf_op jit(solution)/shard_map/reduce_scatter | solution.py:301
  750.3 329.2 %reduce-scatter.35.cloned.1.call-start = ((), (), s32[]{:S(2)}) async-start(), calls=%async_computation.28 | async-start | bytes 10616832 | tf_op jit(solution)/shard_map/reduce_scatter | solution.py:74
  761.2 484.1 %reduce-scatter.31.cloned.1.call-start = ((), (), s32[]{:S(2)}) async-start(), calls=%async_computation.26 | async-start | bytes 10616832 | tf_op jit(solution)/shard_map/reduce_scatter | solution.py:73
  773.4 493.6 %reduce-scatter.39.cloned.1.call-start = ((), (), s32[]{:S(2)}) async-start(), calls=%async_computation.30 | async-start | bytes 245760
  799.4 600.2 %reduce-scatter.37.cloned.1.call-start = ((), (), s32[]{:S(2)}) async-start(), calls=%async_computation.29 | async-start | bytes 7962624
  930.0 157.6 %copy-start.45 = (f32[768]{0:T(1024)S(1)}, f32[768]{0:T(1024)}, u32[]{:S(2)}) copy-start(f32[768]{0:T(1024)} %get-tuple-element.125) | copy-start | bytes 9220
  930.0 157.6 %copy-start.51 = (f32[3072]{0:T(1024)S(1)}, f32[3072]{0:T(1024)}, u32[]{:S(2)}) copy-start(f32[3072]{0:T(1024)} %get-tuple-element.181) | copy-start | bytes 36868
  930.0 157.6 %copy-start.52 = (f32[3072]{0:T(1024)S(1)}, f32[3072]{0:T(1024)}, u32[]{:S(2)}) copy-start(f32[3072]{0:T(1024)} %get-tuple-element.183) | copy-start | bytes 36868
  930.0 157.6 %copy-start.54 = (f32[768]{0:T(1024)S(1)}, f32[768]{0:T(1024)}, u32[]{:S(2)}) copy-start(f32[768]{0:T(1024)} %get-tuple-element.101) | copy-start | bytes 9220
  930.0 157.6 %copy-start.57 = (f32[768]{0:T(1024)S(1)}, f32[768]{0:T(1024)}, u32[]{:S(2)}) copy-start(f32[768]{0:T(1024)} %get-tuple-element.154) | copy-start | bytes 9220
  930.0 157.6 %copy-start.53 = (f32[768]{0:T(1024)S(1)}, f32[768]{0:T(1024)}, u32[]{:S(2)}) copy-start(f32[768]{0:T(1024)} %get-tuple-element.90) | copy-start | bytes 9220
  930.0 157.6 %copy-start.56 = (f32[768]{0:T(1024)S(1)}, f32[768]{0:T(1024)}, u32[]{:S(2)}) copy-start(f32[768]{0:T(1024)} %get-tuple-element.157) | copy-start | bytes 9220
  930.0 157.6 %copy-start.47 = (f32[768]{0:T(1024)S(1)}, f32[768]{0:T(1024)}, u32[]{:S(2)}) copy-start(f32[768]{0:T(1024)} %get-tuple-element.129) | copy-start | bytes 9220
  930.0 157.6 %copy-start.55 = (f32[768]{0:T(1024)S(1)}, f32[768]{0:T(1024)}, u32[]{:S(2)}) copy-start(f32[768]{0:T(1024)} %get-tuple-element.131) | copy-start | bytes 9220
  930.1 521.8 %reduce-scatter.41.cloned.1.call-start = ((), (), s32[]{:S(2)}) async-start(), calls=%async_computation.31 | async-start | bytes 737280
  1081.6 165.9 %copy-start.12 = (bf16[1,1,512,768]{3,2,1,0:T(8,128)(2,1)S(1)}, bf16[1,1,512,768]{3,2,1,0:T(8,128)(2,1)}, u32[]{:S(2)}) copy-start(bf16[1,1,512,768]{3,2,1,0:T(8,128)(2,1)} %get-tuple-element.142) | copy-start | bytes 2359300
  1083.9 369.9 %reduce-scatter.33.cloned.1.call-start = ((), (), s32[]{:S(2)}) async-start(), calls=%async_computation.27 | async-start | bytes 737280 | tf_op jit(solution)/shard_map/reduce_scatter | solution.py:95
  1247.5 225.1 %reduce-scatter.27.cloned.1.call-start = ((), (), s32[]{:S(2)}) async-start(), calls=%async_computation.24 | async-start | bytes 737280 | tf_op jit(solution)/shard_map/reduce_scatter | solution.py:89
  (56 other events, 1374.9 us)
Sparse Core Ops, SparseCore 0:
  17.6 66.7 all-gather.10
  94.3 62.2 all-gather.14
  158.1 62.0 all-gather.12
  222.8 39.7 all-gather.16
  264.5 62.2 all-gather.24
  328.8 62.1 all-gather.22
  393.1 78.5 all-gather.18
  473.7 79.1 all-gather.20
  596.2 67.2 reduce-scatter.28
  665.7 59.3 reduce-scatter.18
  727.3 60.2 reduce-scatter.20
  789.8 60.2 reduce-scatter.22
  852.4 60.2 reduce-scatter.24
  916.2 163.2 reduce-scatter.34
  1082.9 162.3 reduce-scatter.30
  1248.2 18.8 reduce-scatter.38
  1270.6 128.9 reduce-scatter.36
  1402.1 21.1 reduce-scatter.40
  1425.9 22.1 reduce-scatter.32
  1450.7 21.9 reduce-scatter.26
where the time goes:
time: 1490 us; the launch traced here: 1480 us
  waiting for transfers between devices  810 us (54%)
  matrix products  375 us (25%)
  blocking collectives  139 us (9%)
  other arithmetic  76.7 us (5%)
  local copies, waits for them, and re-layouts  61 us (4%)
  between operations  19.1 us (1%)
    reduce_scatter x1, waiting for transfers between devices, reduce_rows(): lax.psum_scatter(matrices[2], ('dp', 'seq'), scatter_dimension=0, tiled=T...  158 us
    reduce_scatter x1, waiting for transfers between devices, reduce_rows(): lax.psum_scatter(matrices[3], ('dp', 'seq'), scatter_dimension=0, tiled=T...  149 us
    unnamed x23, waiting for transfers between devices  143 us
    unnamed x2, blocking collectives  74.8 us
    reduce_scatter x2, waiting for transfers between devices, local(): lax.psum_scatter(value_terms.astype(jnp.bfloat16), 'seq', scatter_dimensi...  62.6 us
    dot_general x2, matrix products, local(): jnp.einsum('sqhd,skhd->sqhk', grad_heads, attend_value_piece, preferred_e...  62.3 us
    all_gather x2, waiting for transfers between devices, local(): key_piece = lax.all_gather(keys, 'seq', axis=1, tiled=True)  61 us
    all_gather x1, waiting for transfers between devices, gather_weights(): lax.all_gather(columns[2], ('dp', 'seq'), axis=0, tiled=True)  57.6 us
  transfers between devices with their start and end apart: 20, of which 14 were waited for; matrix products, arithmetic and copies ran while one was open for 30% of the time, Pallas kernels for 0%

commit v1 on v0

--- a/solution.py
+++ b/solution.py
@@ -1,8 +1,9 @@
 import math
-
 import jax
 import jax.numpy as jnp
 from jax import lax
+from jax.experimental import pallas as pl
+from jax.experimental.pallas import tpu as pltpu
 from jax.sharding import PartitionSpec as P
 
 D = 768
@@ -10,6 +11,131 @@
 HEAD = 64
 FF = 3072
 MICRO = 2
+LOG2E = math.log2(math.e)
+NT = (((1,), (1,)), ((), ()))
+TN = (((0,), (0,)), ((), ()))
+f32 = jnp.float32
+bf16 = jnp.bfloat16
+
+
+def dot(a, b, dims=(((1,), (0,)), ((), ()))):
+    return lax.dot_general(a, b, dims, preferred_element_type=f32)
+
+
+def lane_of(shape):
+    return lax.broadcasted_iota(jnp.int32, shape, 1)
+
+
+def attend_kernel(q_ref, k_ref, v_ref, o_ref, qa_ref):
+    rows = q_ref.shape[1]
+    lane = lane_of((rows, 128))
+    halves = []
+    for h in range(2):
+        q = q_ref[h]
+        s = dot(q, k_ref[h], NT)
+        top = jnp.max(s, axis=-1, keepdims=True)
+        p = jnp.exp2(s - top).astype(bf16)
+        o = dot(p, v_ref[h])
+        total = -o[:, 64:65]
+        halves.append(o / total)
+        level = top + jnp.log2(total)
+        high = level.astype(bf16)
+        rest = level - high.astype(f32)
+        mid = rest.astype(bf16)
+        low = (rest - mid.astype(f32)).astype(bf16)
+        qa_ref[h] = jnp.where(
+            lane < 65,
+            q.astype(f32),
+            jnp.where(
+                lane == 65,
+                high.astype(f32),
+                jnp.where(lane == 66, mid.astype(f32), jnp.where(lane == 67, low.astype(f32), 0.0)),
+            ),
+        ).astype(bf16)
+    o_ref[...] = jnp.where(lane < 64, halves[0], pltpu.roll(halves[1], 64, 1)).astype(bf16)
+
+
+def attend(q, k, v, block=512):
+    n, span, _ = q.shape
+    whole = pl.BlockSpec((2, span, 128), lambda p, i: (p, 0, 0))
+    part = pl.BlockSpec((2, block, 128), lambda p, i: (p, i, 0))
+    return pl.pallas_call(
+        attend_kernel,
+        grid=(n // 2, span // block),
+        in_specs=[part, whole, whole],
+        out_specs=[pl.BlockSpec((block, 128), lambda p, i: (i, p)), part],
+        out_shape=[
+            jax.ShapeDtypeStruct((span, n * 64), bf16),
+            jax.ShapeDtypeStruct((n, span, 128), bf16),
+        ],
+        compiler_params=pltpu.CompilerParams(vmem_limit_bytes=56 * 2**20),
+        cost_estimate=pl.CostEstimate(
+            flops=n * span * span * 512, bytes_accessed=n * span * 1024, transcendentals=n * span * span
+        ),
+        name="attend",
+    )(q, k, v)
+
+
+def attend_back_kernel(q_ref, k_ref, v_ref, o_ref, g_ref, dq_ref, dk_ref, dv_ref, ga_ref, acc_ref):
+    step = pl.program_id(1)
+    span = q_ref.shape[1]
+    rows = k_ref.shape[1]
+
+    @pl.when(step == 0)
+    def _():
+        lane = lane_of((span, 128))
+        grad = g_ref[...].astype(f32)
+        prod = grad * o_ref[...].astype(f32)
+        for h in range(2):
+            mine = (lane < 64) if h == 0 else (lane >= 64)
+            delta = jnp.sum(jnp.where(mine, prod, 0.0), axis=-1, keepdims=True)
+            high = delta.astype(bf16).astype(f32)
+            mid = delta - high
+            g = grad if h == 0 else pltpu.roll(grad, 64, 1)
+            ga_ref[h] = jnp.where(
+                lane < 64, g, jnp.where(lane == 64, high, jnp.where(lane == 65, mid, 0.0))
+            ).astype(bf16)
+        acc_ref[...] = jnp.zeros_like(acc_ref)
+
+    lane = lane_of((rows, 128))
+    dks, dvs = [], []
+    for h in range(2):
+        q = q_ref[h]
+        k = k_ref[h]
+        g = ga_ref[h]
+        p = jnp.exp2(dot(k, q, NT))
+        ds = (p * dot(v_ref[h], g, NT)).astype(bf16)
+        dvs.append(dot(p.astype(bf16), g))
+        dks.append(dot(ds, q))
+        acc_ref[h] += dot(ds, k, TN)
+    dk_ref[...] = (jnp.where(lane < 64, dks[0], pltpu.roll(dks[1], 64, 1)) * (1.0 / LOG2E)).astype(bf16)
+    dv_ref[...] = jnp.where(lane < 64, dvs[0], pltpu.roll(dvs[1], 64, 1)).astype(bf16)
+
+    @pl.when(step == pl.num_programs(1) - 1)
+    def _():
+        wide = lane_of((span, 128))
+        dq_ref[...] = (jnp.where(wide < 64, acc_ref[0], pltpu.roll(acc_ref[1], 64, 1)) * 0.125).astype(bf16)
+
+
+def attend_back(q, k, v, o, g, block=256):
+    n, span, _ = q.shape
+    whole = pl.BlockSpec((2, span, 128), lambda p, i: (p, 0, 0))
+    part = pl.BlockSpec((2, block, 128), lambda p, i: (p, i, 0))
+    flat = pl.BlockSpec((span, 128), lambda p, i: (0, p))
+    rows = pl.BlockSpec((block, 128), lambda p, i: (i, p))
+    return pl.pallas_call(
+        attend_back_kernel,
+        grid=(n // 2, span // block),
+        in_specs=[whole, part, part, flat, flat],
+        out_specs=[flat, rows, rows],
+        out_shape=[jax.ShapeDtypeStruct((span, n * 64), bf16)] * 3,
+        scratch_shapes=[pltpu.VMEM((2, span, 128), bf16), pltpu.VMEM((2, span, 128), f32)],
+        compiler_params=pltpu.CompilerParams(vmem_limit_bytes=56 * 2**20),
+        cost_estimate=pl.CostEstimate(
+            flops=n * span * span * 1280, bytes_accessed=n * span * 1024, transcendentals=n * span * span
+        ),
+        name="attend_back",
+    )(q, k, v, o, g)
 
 
 epsilon = 1e-05
@@ -349,42 +475,281 @@
     )
 
 
+def project_kernel(x_ref, w_ref, b_ref, aux_ref, q_ref, k_ref, v_ref):
+    rows = x_ref.shape[0]
+    lane = lane_of((rows, 128))
+    y = dot(x_ref[...], w_ref[0]) + b_ref[0]
+    one = jnp.where(lane == 64, 1.0, 0.0)
+    both = y[:, :128]
+    q_ref[0] = jnp.where(lane < 64, both * (LOG2E / 8.0), one).astype(bf16)
+    k_ref[0] = jnp.where(lane < 64, pltpu.roll(both, 64, 1), aux_ref[...].astype(f32)).astype(bf16)
+    v_ref[0] = jnp.where(lane < 64, y[:, 128:], -1.0).astype(bf16)
+
+
+def project(x, w, b, aux):
+    span = x.shape[0]
+    n = w.shape[0]
+    head = pl.BlockSpec((1, span, 128), lambda h: (h, 0, 0))
+    return pl.pallas_call(
+        project_kernel,
+        grid=(n,),
+        in_specs=[
+            pl.BlockSpec((span, D), lambda h: (0, 0)),
+            pl.BlockSpec((1, D, 256), lambda h: (h, 0, 0)),
+            pl.BlockSpec((1, 1, 256), lambda h: (h, 0, 0)),
+            pl.BlockSpec((span, 128), lambda h: (0, 0)),
+        ],
+        out_specs=[head] * 3,
+        out_shape=[jax.ShapeDtypeStruct((n, span, 128), bf16)] * 3,
+        compiler_params=pltpu.CompilerParams(vmem_limit_bytes=56 * 2**20),
+        cost_estimate=pl.CostEstimate(
+            flops=n * span * D * 512, bytes_accessed=n * span * 768, transcendentals=0
+        ),
+        name="project",
+    )(x, w, b, aux)
+
+
+AXES = ("dp", "seq", "y", "c")
+SWAP = [(0, 1), (1, 0)]
+
+
+def piece_routes(pairs):
+    first, second = [], []
+    for z in range(4):
+        for y in range(pairs):
+            for c in range(2):
+                source = (z * pairs + y) * 2 + c
+                for micro in range(2):
+                    target = ((2 * micro + c) * pairs + y) * 2 + z // 2
+                    (first if micro == z % 2 else second).append((source, target))
+    return first, second
+
+
+def back(route):
+    return [(target, source) for source, target in route]
+
+
+def local_pairs(
+    tokens,
+    lengths,
+    in_weight,
+    in_bias,
+    out_weight,
+    out_bias,
+    mid_gain,
+    mid_shift,
+    up_weight,
+    up_bias,
+    down_weight,
+    down_bias,
+    last_gain,
+    last_shift,
+    grad_output,
+):
+    rows = tokens.shape[2]
+    pairs = lax.axis_size("y")
+    blocks = lax.axis_size("dp") * lax.axis_size("seq")
+    z = lax.axis_index("seq")
+    y = lax.axis_index("y")
+    c = lax.axis_index("c")
+    odd = z % 2
+    route_a, route_b = piece_routes(pairs)
+    where_to = ("seq", "y", "c")
+
+    def spread(array):
+        own = lax.dynamic_index_in_dim(array[:, 0], odd, 0, keepdims=False)
+        other = lax.dynamic_index_in_dim(array[:, 0], 1 - odd, 0, keepdims=False)
+        return jnp.concatenate(
+            [lax.ppermute(own, where_to, route_a), lax.ppermute(other, where_to, route_b)], axis=0
+        )
+
+    def collect(array):
+        own = lax.ppermute(array[:rows], where_to, back(route_a))
+        other = lax.ppermute(array[rows:], where_to, back(route_b))
+        return jnp.stack(
+            [jnp.where(odd == 0, own, other), jnp.where(odd == 0, other, own)], axis=0
+        )[:, None]
+
+    def swap(array):
+        return lax.ppermute(array, "c", SWAP)
+
+    vectors = (in_bias, out_bias, mid_gain, mid_shift, up_bias, down_bias, last_gain, last_shift)
+    x = spread(tokens)
+    packed = lax.all_gather(jnp.concatenate(vectors), ("dp", "seq"), axis=0, tiled=False)
+    whole = []
+    at = 0
+    for v in vectors:
+        whole.append(packed[:, at : at + v.shape[0]].reshape(-1).astype(f32))
+        at += v.shape[0]
+    in_vector, out_vector, mid_scale, mid_offset, up_vector, down_vector, last_scale, last_offset = whole
+
+    w_in = lax.all_gather(in_weight, ("dp", "seq", "y"), axis=0, tiled=False)
+    w_in = w_in.reshape(blocks, pairs, D // blocks, 3, 3, HEAD)
+    n = pairs * 3
+
+    def columns(weight):
+        full = lax.all_gather(weight, AXES, axis=0, tiled=False)
+        full = full.reshape(blocks, 2 * pairs, weight.shape[0], weight.shape[1])
+        return full.transpose(0, 2, 1, 3).reshape(blocks * weight.shape[0], -1)
+
+    w_out = columns(out_weight)
+    w_up = columns(up_weight)
+    w_down = columns(down_weight)
+    g_top = spread(grad_output)
+
+    micro = z // 2
+    group = (lax.axis_index("dp") * pairs + y) * 2 + odd
+    length = lengths[micro, group]
+    iota = jnp.arange(rows, dtype=jnp.int32)
+
+    def places(core):
+        return [(2 * core + micro) * rows + iota, (2 * core + 1 - micro) * rows + iota]
+
+    place = jnp.concatenate(places(c) + places(1 - c))
+    mask = jnp.where(place < length, 0.0, -1e30).astype(bf16)
+    span = 4 * rows
+    half = 2 * rows
+    lane = jnp.arange(128, dtype=jnp.int32)[None, :]
+    aux = jnp.where(
+        lane == 64, mask[:, None], jnp.where((lane > 64) & (lane < 68), -1.0, 0.0).astype(bf16)
+    )
+
+    x_full = jnp.concatenate([x, swap(x)], axis=0)
+    w_head = jnp.pad(
+        w_in.transpose(1, 3, 0, 2, 4, 5).reshape(n, D, 192), ((0, 0), (0, 0), (0, 64))
+    )
+    bias = lax.dynamic_index_in_dim(
+        in_vector.reshape(pairs, 2, 3, 2, HEAD), c, 1, keepdims=False
+    ).reshape(n, 2, HEAD)
+    b_head = jnp.concatenate(
+        [bias[:, 0], jnp.zeros_like(bias[:, 0]), bias[:, 1], jnp.zeros_like(bias[:, 0])], axis=1
+    )[:, None]
+    q, k, v = project(x_full, w_head, b_head, aux)
+    attended, q = attend(q, k, v)
+    mine = attended[:half]
+    theirs = swap(attended[half:])
+
+    def by_core(own, other):
+        even = jnp.where(c == 0, own, other).reshape(half, pairs, 1, 192)
+        odd_ = jnp.where(c == 0, other, own).reshape(half, pairs, 1, 192)
+        return jnp.concatenate([even, odd_], axis=2).reshape(half, D)
+
+    att = by_core(mine, theirs)
+    mixed = dot(att, w_out) + out_vector
+    first_std, first_scale = standardize(x.astype(f32) + mixed)
+    normed = first_std * mid_scale + mid_offset
+    normed_low = normed.astype(bf16)
+    pre_up = dot(normed_low, w_up) + up_vector
+    act_low = jax.nn.gelu(pre_up, approximate=False).astype(bf16)
+    branch = dot(act_low, w_down) + down_vector
+    second_std, second_scale = standardize(normed + branch)
+    result = collect((second_std * last_scale + last_offset).astype(bf16))
+
+    g_top = g_top.astype(f32)
+    vec_last_gain = jnp.sum(g_top * second_std, axis=0)
+    vec_last_shift = jnp.sum(g_top, axis=0)
+    grad_second = norm_back(g_top, second_std, second_scale, last_scale)
+    grad_branch = grad_second.astype(bf16)
+    vec_down = row_sum(grad_branch)
+    grad_down = dot(act_low, grad_branch, TN)
+    grad_pre = (dot(grad_branch, w_down, NT) * gelu_slope(pre_up)).astype(bf16)
+    vec_up = row_sum(grad_pre)
+    grad_up = dot(normed_low, grad_pre, TN)
+    grad_normed = grad_second + dot(grad_pre, w_up, NT)
+    vec_mid_gain = jnp.sum(grad_normed * first_std, axis=0)
+    vec_mid_shift = jnp.sum(grad_normed, axis=0)
+    grad_first = norm_back(grad_normed, first_std, first_scale, mid_scale)
+    grad_mixed = grad_first.astype(bf16)
+    vec_out = row_sum(grad_mixed)
+    grad_out = dot(att, grad_mixed, TN)
+    grad_att = dot(grad_mixed, w_out, NT).astype(bf16).reshape(half, pairs, 2, 192)
+    g_even = grad_att[:, :, 0].reshape(half, n * HEAD)
+    g_odd = grad_att[:, :, 1].reshape(half, n * HEAD)
+    g_own = jnp.where(c == 0, g_even, g_odd)
+    g_other = swap(jnp.where(c == 0, g_odd, g_even))
+    dq, dk, dv = attend_back(q, k, v, attended, jnp.concatenate([g_own, g_other], axis=0))
+
+    def scatter(grad, weight):
+        r, w = weight.shape
+        grad = grad.astype(bf16).reshape(blocks, r, 2 * pairs, w).transpose(0, 2, 1, 3)
+        return lax.psum_scatter(
+            grad.reshape(2 * pairs * blocks, r, w), AXES, scatter_dimension=0, tiled=True
+        )[0].astype(f32)
+
+    out_down = scatter(grad_down, down_weight)
+    out_up = scatter(grad_up, up_weight)
+    out_out = scatter(grad_out, out_weight)
+    grad_proj = jnp.concatenate([dq, dk, dv], axis=1)
+    grad_in = dot(x_full, grad_proj, TN).astype(bf16)
+    r = in_weight.shape[0]
+    grad_in = grad_in.reshape(blocks, r, 3, pairs, 192).transpose(0, 3, 1, 2, 4)
+    out_in = lax.psum_scatter(
+        grad_in.reshape(blocks * pairs, r, 576), ("dp", "seq", "y"), scatter_dimension=0, tiled=True
+    )[0]
+    out_in = out_in.reshape(r, 3, 3, HEAD).transpose(0, 2, 1, 3).reshape(r, 576).astype(f32)
+    w_kind = w_in.transpose(0, 2, 4, 1, 3, 5).reshape(D, 3 * n * HEAD)
+    grad_x = dot(grad_proj, w_kind, NT)
+    grad_x = grad_first + grad_x[:half] + swap(grad_x[half:].astype(bf16)).astype(f32)
+    grad_tokens = collect(grad_x.astype(bf16)).astype(f32)
+    own_bias = jnp.stack(
+        [row_sum(dq).reshape(pairs, 3, HEAD), row_sum(dv).reshape(pairs, 3, HEAD)], axis=2
+    )
+    core = (jnp.arange(2) == c).astype(f32)
+    vec_in = (own_bias[:, None] * core[None, :, None, None, None]).reshape(-1)
+    grads = (
+        vec_in,
+        vec_out,
+        vec_mid_gain,
+        vec_mid_shift,
+        vec_up,
+        vec_down,
+        vec_last_gain,
+        vec_last_shift,
+    )
+    packed = jnp.concatenate([g.reshape(blocks, -1) for g in grads], axis=1)
+    total = lax.psum(packed, AXES)
+    total = lax.dynamic_index_in_dim(
+        total, lax.axis_index("dp") * lax.axis_size("seq") + z, 0, keepdims=False
+    )
+    sums = []
+    at = 0
+    for vector in vectors:
+        sums.append(total[at : at + vector.shape[0]])
+        at += vector.shape[0]
+    return (
+        result,
+        grad_tokens,
+        out_in,
+        sums[0],
+        out_out,
+        sums[1],
+        sums[2],
+        sums[3],
+        out_up,
+        sums[4],
+        out_down,
+        sums[5],
+        sums[6],
+        sums[7],
+    )
+
+
+def specs(fsdp):
+    data = P(None, ("dp",) + fsdp, "seq", None)
+    matrix = P(("dp", "seq"), fsdp)
+    vector = P(("dp", "seq"))
+    ins = (data, P(), matrix, vector, matrix, vector, vector, vector, matrix, vector, matrix, vector)
+    ins += (vector, vector, data)
+    outs = (data, data, matrix, vector, matrix, vector, vector, vector, matrix, vector, matrix)
+    outs += (vector, vector, vector)
+    return ins, outs
+
+
 def solution(mesh):
-    return jax.shard_map(
-        local,
-        mesh=mesh,
-        in_specs=(
-            P(None, ("dp", "fsdp"), "seq", None),
-            P(),
-            P(("dp", "seq"), "fsdp"),
-            P(("dp", "seq")),
-            P(("dp", "seq"), "fsdp"),
-            P(("dp", "seq")),
-            P(("dp", "seq")),
-            P(("dp", "seq")),
-            P(("dp", "seq"), "fsdp"),
-            P(("dp", "seq")),
-            P(("dp", "seq"), "fsdp"),
-            P(("dp", "seq")),
-            P(("dp", "seq")),
-            P(("dp", "seq")),
-            P(None, ("dp", "fsdp"), "seq", None),
-        ),
-        out_specs=(
-            P(None, ("dp", "fsdp"), "seq", None),
-            P(None, ("dp", "fsdp"), "seq", None),
-            P(("dp", "seq"), "fsdp"),
-            P(("dp", "seq")),
-            P(("dp", "seq"), "fsdp"),
-            P(("dp", "seq")),
-            P(("dp", "seq")),
-            P(("dp", "seq")),
-            P(("dp", "seq"), "fsdp"),
-            P(("dp", "seq")),
-            P(("dp", "seq"), "fsdp"),
-            P(("dp", "seq")),
-            P(("dp", "seq")),
-            P(("dp", "seq")),
-        ),
-        check_vma=False,
-    )
+    dp, seq, fsdp = (mesh.shape[name] for name in ("dp", "seq", "fsdp"))
+    if seq == 2 * MICRO and fsdp % 2 == 0:
+        mesh = jax.sharding.Mesh(mesh.devices.reshape(dp, seq, fsdp // 2, 2), AXES)
+        body, (ins, outs) = local_pairs, specs(("y", "c"))
+    else:
+        body, (ins, outs) = local, specs(("fsdp",))
+    return jax.shard_map(body, mesh=mesh, in_specs=ins, out_specs=outs, check_vma=False)

time: 1490 us -> 862 us (0.58)
  waiting for transfers between devices: 810 us -> 273 us
  matrix products: 375 us -> 100 us
  Pallas kernels: 0 us -> 138 us
  local copies, waits for them, and re-layouts: 61 us -> 146 us
  other arithmetic: 76.7 us -> 33.8 us
  starting transfers between devices: 1.29 us -> 25.2 us
  blocking collectives: 139 us -> 120 us
    dot_general x36 -> x11, matrix products: 375 us -> 100 us  [dot(): return lax.dot_general(a, b, dims, preferred_element_type=f32)]
    reduce_scatter x9 -> x4, waiting for transfers between devices: 429 us -> 174 us  [the longest x3 174 us: scatter(): lax.psum_scatter(grad.reshape(2 * pairs * blocks, r, w), AXES, scatter_di...]
    all_gather x8 -> x4, waiting for transfers between devices: 238 us -> 64.5 us  [the longest x3 64.5 us: columns(): full = lax.all_gather(weight, AXES, axis=0, tiled=False)]
    unnamed x23 -> x8, waiting for transfers between devices: 143 us -> 2.65 us
    pallas_call x0 -> x3, Pallas kernels: none -> 138 us  [the longest x1 79.6 us: attend_back(): pl.pallas_call(attend_back_kernel, grid=(n // 2, span // block), in_specs...]
    reshape x1 -> x20, local copies, waits for them, and re-layouts: 0.09 us -> 77 us  [the longest x4 19.3 us: columns(): full = full.reshape(blocks, 2 * pairs, weight.shape[0], weight.shape[1])]
    unnamed x2 -> x0, blocking collectives: 74.8 us -> none
    reduce_sum x6 -> x1, other arithmetic: 52.6 us -> 3.42 us  [local_pairs(): vec_last_gain = jnp.sum(g_top * second_std, axis=0)]
  transfers between devices with their start and end apart: 20 -> 20, of which waited for: 14 -> 6; matrix products, arithmetic and copies ran while one was open for 30% -> 28% of each run, Pallas kernels for 0% -> 16%
where the time goes in v1:
time: 862 us; the launch traced here: 851 us
  waiting for transfers between devices  273 us (32%)
  local copies, waits for them, and re-layouts  146 us (17%)
  Pallas kernels  138 us (16%)
  blocking collectives  120 us (14%)
  matrix products  100 us (12%)
  other arithmetic  33.8 us (4%)
  starting transfers between devices  25.2 us (3%)
  between operations  15 us (2%)
    reduce_scatter x3, waiting for transfers between devices, scatter(): lax.psum_scatter(grad.reshape(2 * pairs * blocks, r, w), AXES, scatter_di...  174 us
    dot_general x11, matrix products, dot(): return lax.dot_general(a, b, dims, preferred_element_type=f32)  100 us
    pallas_call x1, Pallas kernels, attend_back(): pl.pallas_call(attend_back_kernel, grid=(n // 2, span // block), in_specs...  79.6 us
    all_gather x1, blocking collectives, local_pairs(): lax.all_gather(jnp.concatenate(vectors), ('dp', 'seq'), axis=0, tiled=False)  66.2 us
    all_gather x3, waiting for transfers between devices, columns(): full = lax.all_gather(weight, AXES, axis=0, tiled=False)  64.5 us
    psum x1, blocking collectives, local_pairs(): total = lax.psum(packed, AXES)  53.5 us
    pallas_call x1, Pallas kernels, attend(): pl.pallas_call(attend_kernel, grid=(n // 2, span // block), in_specs=[par...  48 us
    ppermute x2, waiting for transfers between devices, collect(): other = lax.ppermute(array[rows:], where_to, back(route_b))  30.5 us
  transfers between devices with their start and end apart: 20, of which 6 were waited for; matrix products, arithmetic and copies ran while one was open for 28% of the time, Pallas kernels for 16%

profile of v1, /device:TPU:0, one launch (start us, length us, event | category | flops | bytes accessed | tf_op | source)
XLA Modules:
  0.0 850.6 jit_solution(12048104060747982872)
XLA Ops:
  12.3 5.3 collective-permute-start.1
  17.8 66.2 %all-gather.5 = bf16[8,1,1152]{2,1,0:T(2,128)(2,1)S(1)} all-gather(bf16[1,1,1152]{2,1,0:T(2,128)(2,1)S(1)} %reshape.387), channel_id=3, replica_groups=mesh['dp'=2,'seq'=4,'y'=2,'c'=2] {'dp','seq'}, dimensions={0}, use_global_device_ids=true | all-gather | bytes 20736 | tf_op jit(solution)/shard_map/all_gather | solution.py:578
  96.5 7.7 reshape.336
  104.2 7.1 copy.112
  111.3 9.5 %reshape.390 = bf16[6,768,192]{2,1,0:T(8,128)(2,1)} reshape(bf16[2,3,8,96,3,64]{5,4,3,2,1,0:T(4,128)(2,1)} %copy.112) | data formatting | bytes 3538944 | tf_op jit(solution)/shard_map/reshape | solution.py:619
  124.2 10.2 %project.1 = (bf16[6,2048,128]{2,1,0:T(8,128)(2,1)}, bf16[6,2048,128]{2,1,0:T(8,128)(2,1)}, bf16[6,2048,128]{2,1,0:T(8,128)(2,1)}) custom-call(bf16[2048,768]{1,0:T(8,128)(2,1)} %constant_dynamic-update-slice_fusion.2.x_ref, bf16[6,768,256]{2,1,0:T(8,128)(2,1)} %pad.4.w_ref, f32[6,1,256]{2,1,0:T(1,128)} %broadcast_in_dim.44.b_ref, ...), custom_call_target="tpu_custom_call" | custom-call | flops 4831838208 | bytes 9437184 | tf_op jit(solution)/shard_map/project/pallas_call | solution.py:493
  134.4 48.0 %attend.1 = (bf16[2048,384]{1,0:T(8,128)(2,1)}, bf16[6,2048,128]{2,1,0:T(8,128)(2,1)}) custom-call(bf16[6,2048,128]{2,1,0:T(8,128)(2,1)} %get-tuple-element.22.q_ref, bf16[6,2048,128]{2,1,0:T(8,128)(2,1)} %get-tuple-element.23.k_ref, bf16[6,2048,128]{2,1,0:T(8,128)(2,1)} %get-tuple-element.24.v_ref), custom_call_target="tpu_custom_call" | custom-call | flops 12884901888 | bytes 12582912 | tf_op jit(solution)/shard_map/attend/pallas_call | solution.py:62
  185.4 7.4 collective-permute-start.6
  208.0 6.0 copy.96
  217.2 61.0 %all-gather.17.cloned.1.call-done = bf16[12288,192]{0,1:T(8,128)(2,1)} async-done(((bf16[384,192]{0,1:T(8,128)(2,1)}), bf16[12288,192]{0,1:T(8,128)(2,1)}) %all-gather.17.cloned.1.call-update) | async-done | bytes 4718608 | tf_op jit(solution)/shard_map/all_gather | solution.py:591
  278.2 8.2 reshape.346
  290.7 34.8 %fusion.2 = (bf16[1024,3072]{1,0:T(8,128)(2,1)S(1)}, f32[1024,3072]{1,0:T(8,128)}) fusion(f32[3072]{0:T(1024)S(1)} %reshape.369, bf16[768,3072]{1,0:T(8,128)(2,1)S(1)} %bitcast.148, f32[1024,768]{1,0:T(8,128)S(1)} %get-tuple-element.134, f32[768]{0:T(1024)S(1)} %reshape.368, f32[768]{0:T(1024)S(1)} %reshape.367, f32[1024]{0:T(1024)S(1)} %add_rsqrt_fusion.1, ...), kind=kOutput, calls=%fused_computation.4 | convolution fusion | flops 5043388416 | bytes 26765312 | tf_op jit(solution)/shard_map/dot_general | solution.py:22
  325.6 5.4 fusion.39
  339.0 13.3 %convert_reduce_fusion = (f32[3072]{0:T(1024)S(1)}, bf16[1024,3072]{1,0:T(8,128)(2,1)S(1)}) fusion(f32[1024,3072]{1,0:T(8,128)} %get-tuple-element.136, f32[3072]{0:T(1024)S(1)} %reshape.369, bf16[3072,768]{0,1:T(8,128)(2,1)S(1)} %bitcast.151, f32[1024,768]{1,0:T(8,128)S(1)} %get-tuple-element.95), kind=kOutput, calls=%fused_computation.11 | convolution fusion | flops 4873516032 | bytes 26763264 | tf_op jit(solution)/shard_map/dot_general | solution.py:22
  352.3 6.0 multiply_reduce_fusion
  365.0 4.7 convolution_convert_fusion.4
  369.8 4.4 reshape.359
  382.1 79.6 %attend_back.1 = (bf16[2048,384]{1,0:T(8,128)(2,1)}, bf16[2048,384]{1,0:T(8,128)(2,1)}, bf16[2048,384]{1,0:T(8,128)(2,1)}) custom-call(bf16[6,2048,128]{2,1,0:T(8,128)(2,1)} %get-tuple-element.26.q_ref, bf16[6,2048,128]{2,1,0:T(8,128)(2,1)} %get-tuple-element.23.k_ref, bf16[6,2048,128]{2,1,0:T(8,128)(2,1)} %get-tuple-element.24.v_ref, ...), custom_call_target="tpu_custom_call" | custom-call | flops 32212254720 | bytes 12582912 | tf_op jit(solution)/shard_map/attend_back/pallas_call | solution.py:126
  466.6 5.5 convolution_convert_fusion.2
  472.2 6.6 reshape.350
  478.7 6.4 copy.103
  485.2 9.7 %convolution_convert_fusion = bf16[3072,768]{1,0:T(8,128)(2,1)} fusion(bf16[1024,3072]{1,0:T(8,128)(2,1)} %copy-done.25, f32[1024,768]{1,0:T(8,128)} %copy-done.6), kind=kOutput, calls=%fused_computation.27 | convolution fusion | flops 4834983936 | bytes 14155776 | tf_op jit(solution)/shard_map/dot_general | solution.py:22
  494.9 6.7 copy.107
  508.3 10.1 %convolution_convert_fusion.1 = bf16[768,3072]{1,0:T(8,128)(2,1)} fusion(bf16[1024,3072]{1,0:T(8,128)(2,1)} %copy-done.24, f32[1024,768]{1,0:T(8,128)S(1)} %get-tuple-element.134, f32[768]{0:T(1024)S(1)} %reshape.368, f32[768]{0:T(1024)S(1)} %reshape.367, f32[1024]{0:T(1024)S(1)} %add_rsqrt_fusion.1, f32[1024]{0:T(1024)S(1)} %broadcast_multiply_fusion.6), kind=kOutput, calls=%fused_computation.28 | convolution fusion | flops 4838129664 | bytes 14170112 | tf_op jit(solution)/shard_map/dot_general | solution.py:22
  518.4 9.8 %reshape.361 = bf16[8,96,4,768]{3,2,1,0:T(4,128)(2,1)} reshape(bf16[768,3072]{1,0:T(8,128)(2,1)} %convolution_convert_fusion.1) | data formatting | bytes 9437184 | tf_op jit(solution)/shard_map/reshape | solution.py:674
  528.2 5.4 copy.106
  540.9 6.1 fusion.40
  554.5 7.4 collective-permute-start.4
  565.9 53.5 %psum.7 = f32[8,1152]{1,0:T(8,128)S(1)} all-reduce(f32[8,1152]{1,0:T(8,128)S(1)} %concatenate.51), channel_id=1, replica_groups=mesh['dp'=2,'seq'=4,'y'=2,'c'=2] {'dp','seq','y','c'}, use_global_device_ids=true, to_apply=%region_18.19 | all-reduce | flops 9216 | bytes 73728 | tf_op jit(solution)/shard_map/psum | solution.py:710
  631.5 30.5 %collective-permute-done.11 = bf16[512,768]{1,0:T(8,128)(2,1)S(1)} collective-permute-done((bf16[512,768]{1,0:T(8,128)(2,1)S(1)}, bf16[512,768]{1,0:T(8,128)(2,1)S(1)}, u32[]{:S(2)}, u32[]{:S(2)}) %collective-permute-start.11) | collective-permute-done | bytes 786464 | tf_op jit(solution)/shard_map/ppermute | solution.py:568
  665.9 64.4 %reduce-scatter.11.cloned.1.call-done = bf16[1,384,192]{1,2,0:T(8,128)(2,1)} async-done(((bf16[32,384,192]{1,2,0:T(8,128)(2,1)}), bf16[1,384,192]{1,2,0:T(8,128)(2,1)}) %reduce-scatter.11.cloned.1.call-update) | async-done | bytes 147472 | tf_op jit(solution)/shard_map/reduce_scatter | solution.py:675
  731.9 110.0 %reduce-scatter.9.cloned.1.call-done = bf16[1,96,768]{2,1,0:T(8,128)(2,1)} async-done(((bf16[32,96,768]{2,1,0:T(8,128)(2,1)}), bf16[1,96,768]{2,1,0:T(8,128)(2,1)}) %reduce-scatter.9.cloned.1.call-update) | async-done | bytes 147472 | tf_op jit(solution)/shard_map/reduce_scatter | solution.py:675
  (203 shorter events, 118.5 us)
Async XLA Ops:
  7.2 10.5 %copy-start.16 = (bf16[192]{0:T(256)(128)(2,1)S(1)}, bf16[192]{0:T(256)(128)(2,1)}, u32[]{:S(2)}) copy-start(bf16[192]{0:T(256)(128)(2,1)} %param.18) | copy-start | bytes 1156
  7.2 10.5 %copy-start.17 = (bf16[96]{0:T(256)(128)(2,1)S(1)}, bf16[96]{0:T(256)(128)(2,1)}, u32[]{:S(2)}) copy-start(bf16[96]{0:T(256)(128)(2,1)} %param.20) | copy-start | bytes 580
  7.2 10.4 %copy-start.18 = (bf16[96]{0:T(256)(128)(2,1)S(1)}, bf16[96]{0:T(256)(128)(2,1)}, u32[]{:S(2)}) copy-start(bf16[96]{0:T(256)(128)(2,1)} %param.21) | copy-start | bytes 580
  7.2 10.4 %copy-start.19 = (bf16[96]{0:T(256)(128)(2,1)S(1)}, bf16[96]{0:T(256)(128)(2,1)}, u32[]{:S(2)}) copy-start(bf16[96]{0:T(256)(128)(2,1)} %param.22) | copy-start | bytes 580
  7.2 10.4 %copy-start.15 = (bf16[384]{0:T(512)(128)(2,1)S(1)}, bf16[384]{0:T(512)(128)(2,1)}, u32[]{:S(2)}) copy-start(bf16[384]{0:T(512)(128)(2,1)} %param.24) | copy-start | bytes 2308
  7.2 10.4 %copy-start.20 = (bf16[96]{0:T(256)(128)(2,1)S(1)}, bf16[96]{0:T(256)(128)(2,1)}, u32[]{:S(2)}) copy-start(bf16[96]{0:T(256)(128)(2,1)} %param.26) | copy-start | bytes 580
  7.2 10.4 %copy-start.21 = (bf16[96]{0:T(256)(128)(2,1)S(1)}, bf16[96]{0:T(256)(128)(2,1)}, u32[]{:S(2)}) copy-start(bf16[96]{0:T(256)(128)(2,1)} %param.27) | copy-start | bytes 580
  7.3 10.4 %copy-start.22 = (bf16[96]{0:T(256)(128)(2,1)S(1)}, bf16[96]{0:T(256)(128)(2,1)}, u32[]{:S(2)}) copy-start(bf16[96]{0:T(256)(128)(2,1)} %param.28) | copy-start | bytes 580
  7.3 85.3 %all-gather.11.cloned.1.call-start = ((), (), s32[]{:S(2)}) async-start(), calls=%async_computation.8 | async-start | bytes 2088960 | tf_op jit(solution)/shard_map/all_gather | solution.py:586
  8.0 185.6 %all-gather.13.cloned.1.call-start = ((), (), s32[]{:S(2)}) async-start(), calls=%async_computation.9 | async-start | bytes 1622016 | tf_op jit(solution)/shard_map/all_gather | solution.py:591
  8.7 199.2 %all-gather.15.cloned.1.call-start = ((), (), s32[]{:S(2)}) async-start(), calls=%async_computation.10 | async-start | bytes 4866048 | tf_op jit(solution)/shard_map/all_gather | solution.py:591
  9.5 268.7 %all-gather.17.cloned.1.call-start = ((), (), s32[]{:S(2)}) async-start(), calls=%async_computation.11 | async-start | bytes 4866048 | tf_op jit(solution)/shard_map/all_gather | solution.py:591
  10.1 620.0 %reduce-scatter.7.cloned.1.call-start = ((), (), s32[]{:S(2)}) async-start(), calls=%async_computation.5 | async-start | bytes 1622016 | tf_op jit(solution)/shard_map/reduce_scatter | solution.py:675
  11.6 76.8 %copy-start.23 = (s32[2,8]{1,0:T(2,128)S(1)}, s32[2,8]{1,0:T(2,128)}, u32[]{:S(2)}) copy-start(s32[2,8]{1,0:T(2,128)} %param.16) | copy-start | bytes 196
  11.6 72.5 %collective-permute-start = (bf16[512,768]{1,0:T(8,128)(2,1)S(1)}, bf16[512,768]{1,0:T(8,128)(2,1)S(1)}, u32[]{:S(2)}, u32[]{:S(2)}) collective-permute-start(bf16[512,768]{1,0:T(8,128)(2,1)S(1)} %get-tuple-element.114), channel_id=1, source_target_pairs={{0,0},{1,4},{2,2},{3,6},{4,8},{5,12},{6,10},{7,14},{8,1},{9,5},{10... | collective-permute-start | bytes 2359304 | tf_op jit(solution)/shard_map/ppermute | solution.py:563
  12.3 72.7 %collective-permute-start.1 = (bf16[512,768]{1,0:T(8,128)(2,1)S(1)}, bf16[512,768]{1,0:T(8,128)(2,1)S(1)}, u32[]{:S(2)}, u32[]{:S(2)}) collective-permute-start(bf16[512,768]{1,0:T(8,128)(2,1)S(1)} %get-tuple-element.113), channel_id=1, source_target_pairs={{0,8},{1,12},{2,10},{3,14},{4,0},{5,4},{6,2},{7,6},{8,9},{9,13},{1... | collective-permute-start | bytes 2359304 | tf_op jit(solution)/shard_map/ppermute | solution.py:563
  87.7 3.6 collective-permute-start.2
  134.4 49.6 %copy-start.7 = (bf16[2,1,512,768]{3,2,1,0:T(8,128)(2,1)S(1)}, bf16[2,1,512,768]{3,2,1,0:T(8,128)(2,1)}, u32[]{:S(2)}) copy-start(bf16[2,1,512,768]{3,2,1,0:T(8,128)(2,1)} %param.29) | copy-start | bytes 4718596
  183.9 13.9 %collective-permute-start.3 = (bf16[1024,384]{1,0:T(8,128)(2,1)S(1)}, bf16[1024,384]{1,0:T(8,128)(2,1)S(1)}, u32[]{:S(2)}, u32[]{:S(2)}) collective-permute-start(bf16[1024,384]{1,0:T(8,128)(2,1)S(1)} %slice.113), channel_id=1, source_target_pairs={{0,1},{1,0},{2,3},{3,2},{4,5},{5,4},{6,7},{7,6},{8,9},{9,8},{10,11... | collective-permute-start | bytes 2359304 | tf_op jit(solution)/shard_map/ppermute | solution.py:574
  185.4 146.2 %collective-permute-start.6 = (bf16[512,768]{1,0:T(8,128)(2,1)}, bf16[512,768]{1,0:T(8,128)(2,1)}, u32[]{:S(2)}, u32[]{:S(2)}) collective-permute-start(bf16[512,768]{1,0:T(8,128)(2,1)} %get-tuple-element.107), channel_id=1, source_target_pairs={{0,0},{1,4},{2,2},{3,6},{4,8},{5,12},{6,10},{7,14},{8,1},{9,5},{10... | collective-permute-start | bytes 2359304 | tf_op jit(solution)/shard_map/ppermute | solution.py:563
  192.8 138.8 %collective-permute-start.7 = (bf16[512,768]{1,0:T(8,128)(2,1)}, bf16[512,768]{1,0:T(8,128)(2,1)}, u32[]{:S(2)}, u32[]{:S(2)}) collective-permute-start(bf16[512,768]{1,0:T(8,128)(2,1)} %get-tuple-element.108), channel_id=1, source_target_pairs={{0,8},{1,12},{2,10},{3,14},{4,0},{5,4},{6,2},{7,6},{8,9},{9,13},{1... | collective-permute-start | bytes 2359304 | tf_op jit(solution)/shard_map/ppermute | solution.py:563
  339.0 13.3 %copy-start.6 = (f32[1024,768]{1,0:T(8,128)}, f32[1024,768]{1,0:T(8,128)S(1)}, u32[]{:S(2)}) copy-start(f32[1024,768]{1,0:T(8,128)S(1)} %get-tuple-element.95) | copy-start | bytes 9437188
  364.8 14.7 %collective-permute-start.8 = (bf16[1024,384]{1,0:T(8,128)(2,1)}, bf16[1024,384]{1,0:T(8,128)(2,1)}, u32[]{:S(2)}, u32[]{:S(2)}) collective-permute-start(bf16[1024,384]{1,0:T(8,128)(2,1)} %copy.100), channel_id=1, source_target_pairs={{0,1},{1,0},{2,3},{3,2},{4,5},{5,4},{6,7},{7,6},{8,9},{9,8},{10,11... | collective-permute-start | bytes 2359304 | tf_op jit(solution)/shard_map/ppermute | solution.py:574
  377.1 287.0 %reduce-scatter.5.cloned.1.call-start = ((), (), s32[]{:S(2)}) async-start(), calls=%async_computation.4 | async-start | bytes 2506752 | tf_op jit(solution)/shard_map/reduce_scatter | solution.py:686
  485.1 245.2 %reduce-scatter.11.cloned.1.call-start = ((), (), s32[]{:S(2)}) async-start(), calls=%async_computation.7 | async-start | bytes 4866048 | tf_op jit(solution)/shard_map/reduce_scatter | solution.py:675
  508.3 333.6 %reduce-scatter.9.cloned.1.call-start = ((), (), s32[]{:S(2)}) async-start(), calls=%async_computation.6 | async-start | bytes 4866048 | tf_op jit(solution)/shard_map/reduce_scatter | solution.py:675
  551.0 69.7 %collective-permute-start.9 = (bf16[1024,768]{1,0:T(8,128)(2,1)}, bf16[1024,768]{1,0:T(8,128)(2,1)}, u32[]{:S(2)}, u32[]{:S(2)}) collective-permute-start(bf16[1024,768]{1,0:T(8,128)(2,1)} %slice.189), channel_id=1, source_target_pairs={{0,1},{1,0},{2,3},{3,2},{4,5},{5,4},{6,7},{7,6},{8,9},{9,8},{10,11... | collective-permute-start | bytes 4718600 | tf_op jit(solution)/shard_map/ppermute | solution.py:574
  551.7 68.9 %copy-start.3 = (f32[1024,768]{1,0:T(8,128)S(1)}, f32[1024,768]{1,0:T(8,128)}, u32[]{:S(2)}) copy-start(f32[1024,768]{1,0:T(8,128)} %copy-done.2) | copy-start | bytes 9437188
  554.5 72.8 %collective-permute-start.4 = (bf16[512,768]{1,0:T(8,128)(2,1)}, bf16[512,768]{1,0:T(8,128)(2,1)}, u32[]{:S(2)}, u32[]{:S(2)}) collective-permute-start(bf16[512,768]{1,0:T(8,128)(2,1)} %get-tuple-element.111), channel_id=1, source_target_pairs={{0,0},{4,1},{2,2},{6,3},{8,4},{12,5},{10,6},{14,7},{1,8},{5,9},{3,... | collective-permute-start | bytes 2359304 | tf_op jit(solution)/shard_map/ppermute | solution.py:567
  562.0 65.3 %collective-permute-start.5 = (bf16[512,768]{1,0:T(8,128)(2,1)}, bf16[512,768]{1,0:T(8,128)(2,1)}, u32[]{:S(2)}, u32[]{:S(2)}) collective-permute-start(bf16[512,768]{1,0:T(8,128)(2,1)} %get-tuple-element.112), channel_id=1, source_target_pairs={{8,0},{12,1},{10,2},{14,3},{0,4},{4,5},{2,6},{6,7},{9,8},{13,9},{1... | collective-permute-start | bytes 2359304 | tf_op jit(solution)/shard_map/ppermute | solution.py:568
  623.7 7.9 collective-permute-start.10
  624.4 37.7 %collective-permute-start.11 = (bf16[512,768]{1,0:T(8,128)(2,1)S(1)}, bf16[512,768]{1,0:T(8,128)(2,1)S(1)}, u32[]{:S(2)}, u32[]{:S(2)}) collective-permute-start(bf16[512,768]{1,0:T(8,128)(2,1)S(1)} %get-tuple-element.104), channel_id=1, source_target_pairs={{8,0},{12,1},{10,2},{14,3},{0,4},{4,5},{2,6},{6,7},{9,8},{13,9},{1... | collective-permute-start | bytes 2359304 | tf_op jit(solution)/shard_map/ppermute | solution.py:568
  (16 other events, 47.9 us)
Sparse Core Ops, SparseCore 0:
  10.8 69.6 all-gather.10
  83.4 53.6 all-gather.12
  140.0 67.9 all-gather.14
  210.7 67.4 all-gather.16
  377.2 95.2 reduce-scatter.6
  485.2 132.4 reduce-scatter.4
  624.1 106.1 reduce-scatter.10
  735.8 106.0 reduce-scatter.8

commit v2 on v1

--- a/solution.py
+++ b/solution.py
@@ -475,58 +475,467 @@
     )
 
 
-def project_kernel(x_ref, w_ref, b_ref, aux_ref, q_ref, k_ref, v_ref):
+def half_tiles(first, second):
+    lane = lane_of(first.shape)
+    return jnp.where(lane < 64, first, second)
+
+
+def turn(tile):
+    return pltpu.roll(tile, 64, 1)
+
+
+def join_columns(parts):
+    tiles = []
+    for a, b in (parts[:2], parts[2:]):
+        low = turn(b[:, :128])
+        tiles += [a[:, :128], half_tiles(a[:, 128:], low), half_tiles(low, turn(b[:, 128:]))]
+    return jnp.concatenate(tiles, axis=1)
+
+
+def part_columns(full):
+    parts = []
+    for pair in range(full.shape[1] // 384):
+        t = [full[:, pair * 384 + i * 128 : pair * 384 + i * 128 + 128] for i in range(3)]
+        zero = jnp.zeros_like(t[0])
+        parts.append(jnp.concatenate([t[0], half_tiles(t[1], zero)], axis=1))
+        mid = turn(t[2])
+        parts.append(jnp.concatenate([half_tiles(turn(t[1]), mid), half_tiles(mid, zero)], axis=1))
+    return parts
+
+
+def params(**kw):
+    return pltpu.CompilerParams(vmem_limit_bytes=58 * 2**20, **kw)
+
+
+ANY = pl.BlockSpec(memory_space=pl.ANY)
+
+
+def project_kernel(me_ref, x_ref, b_ref, aux_ref, *rest):
+    pieces, (q_ref, k_ref, v_ref, w_ref, held, sems) = rest[:4], rest[4:]
+    head = pl.program_id(0)
+    xz = me_ref[0]
+
+    def copies():
+        for dx in range(2):
+            for dy in range(2):
+                for dz in range(4):
+                    yield pltpu.make_async_copy(
+                        pieces[dx * 2 + dy].at[dz],
+                        held.at[lax.bitwise_xor(xz, dx * 4 + dz), pl.ds(dy * 3, 3)],
+                        sems.at[dx * 8 + dy * 4 + dz],
+                    )
+
+    @pl.when(head == 0)
+    def _():
+        for copy in copies():
+            copy.start()
+        for copy in copies():
+            copy.wait()
+
     rows = x_ref.shape[0]
     lane = lane_of((rows, 128))
-    y = dot(x_ref[...], w_ref[0]) + b_ref[0]
+    y = dot(x_ref[...], held[:, head].reshape(D, 256)) + b_ref[0]
     one = jnp.where(lane == 64, 1.0, 0.0)
     both = y[:, :128]
     q_ref[0] = jnp.where(lane < 64, both * (LOG2E / 8.0), one).astype(bf16)
-    k_ref[0] = jnp.where(lane < 64, pltpu.roll(both, 64, 1), aux_ref[...].astype(f32)).astype(bf16)
+    k_ref[0] = jnp.where(lane < 64, turn(both), aux_ref[...].astype(f32)).astype(bf16)
     v_ref[0] = jnp.where(lane < 64, y[:, 128:], -1.0).astype(bf16)
 
-
-def project(x, w, b, aux):
+    @pl.when(head == pl.num_programs(0) - 1)
+    def _():
+        for p in range(3):
+            a = held[:, 2 * p].reshape(D, 256).astype(f32)
+            b = held[:, 2 * p + 1].reshape(D, 256).astype(f32)
+            a0, a1, b0, b1 = a[:, :128], a[:, 128:], b[:, :128], b[:, 128:]
+            w_ref[:, p * 128 : p * 128 + 128] = half_tiles(a0, turn(b0)).astype(bf16)
+            w_ref[:, 384 + p * 128 : 512 + p * 128] = half_tiles(turn(a0), b0).astype(bf16)
+            w_ref[:, 768 + p * 128 : 896 + p * 128] = half_tiles(a1, turn(b1)).astype(bf16)
+
+
+def project(me, x, b, aux, pieces):
     span = x.shape[0]
-    n = w.shape[0]
-    head = pl.BlockSpec((1, span, 128), lambda h: (h, 0, 0))
+    n = b.shape[0]
+    head = pl.BlockSpec((1, span, 128), lambda h, m: (h, 0, 0))
     return pl.pallas_call(
         project_kernel,
-        grid=(n,),
-        in_specs=[
-            pl.BlockSpec((span, D), lambda h: (0, 0)),
-            pl.BlockSpec((1, D, 256), lambda h: (h, 0, 0)),
-            pl.BlockSpec((1, 1, 256), lambda h: (h, 0, 0)),
-            pl.BlockSpec((span, 128), lambda h: (0, 0)),
-        ],
-        out_specs=[head] * 3,
-        out_shape=[jax.ShapeDtypeStruct((n, span, 128), bf16)] * 3,
-        compiler_params=pltpu.CompilerParams(vmem_limit_bytes=56 * 2**20),
+        grid_spec=pltpu.PrefetchScalarGridSpec(
+            num_scalar_prefetch=1,
+            grid=(n,),
+            in_specs=[
+                pl.BlockSpec((span, D), lambda h, m: (0, 0)),
+                pl.BlockSpec((1, 1, 256), lambda h, m: (h, 0, 0)),
+                pl.BlockSpec((span, 128), lambda h, m: (0, 0)),
+            ]
+            + [ANY] * 4,
+            out_specs=[head] * 3 + [pl.BlockSpec((D, 1152), lambda h, m: (0, 0))],
+            scratch_shapes=[pltpu.VMEM((8, n, 96, 256), bf16), pltpu.SemaphoreType.DMA((16,))],
+        ),
+        out_shape=[jax.ShapeDtypeStruct((n, span, 128), bf16)] * 3
+        + [jax.ShapeDtypeStruct((D, 1152), bf16)],
+        compiler_params=params(),
         cost_estimate=pl.CostEstimate(
             flops=n * span * D * 512, bytes_accessed=n * span * 768, transcendentals=0
         ),
         name="project",
-    )(x, w, b, aux)
+    )(me, x, b, aux, *pieces)
+
+
+def center(hidden):
+    centered = hidden - jnp.mean(hidden, axis=-1, keepdims=True)
+    scale = lax.rsqrt(jnp.mean(centered * centered, axis=-1, keepdims=True) + epsilon)
+    return centered * scale, scale
+
+
+def middle_kernel(me_ref, x_ref, mine_ref, theirs_ref, g_ref, vec_ref, upb_ref, *rest):
+    up_p, down_p, out_p = rest[:8], rest[8:16], rest[16:24]
+    (
+        y_ref,
+        nl_ref,
+        act_ref,
+        gb_ref,
+        gp_ref,
+        gm_ref,
+        gf_ref,
+        ga_mine_ref,
+        ga_theirs_ref,
+        sum_ref,
+        sum_up_ref,
+        up_w,
+        down_w,
+        out_w,
+        slope,
+        sems,
+    ) = rest[24:]
+    step = pl.program_id(0)
+    xz, my, mc = me_ref[0], me_ref[1], me_ref[2]
+    xor = lax.bitwise_xor
+
+    def copies():
+        for dc in range(2):
+            for dx in range(2):
+                for dy in range(2):
+                    i = dc * 4 + dx * 2 + dy
+                    f = xor(my, dy) * 2 + xor(mc, dc)
+                    for dz in range(4):
+                        at = xor(xz, dx * 4 + dz)
+                        fr = at // 2
+                        pos = xor(fr % 2, mc) * 4 + xor(fr // 2, my) * 2 + at % 2
+                        j = i * 4 + dz
+                        yield pltpu.make_async_copy(out_p[i].at[dz], out_w.at[f, pos], sems.at[0, j])
+                        yield pltpu.make_async_copy(up_p[i].at[dz], up_w.at[f, at], sems.at[1, j])
+                        yield pltpu.make_async_copy(down_p[i].at[dz], down_w.at[at, f], sems.at[2, j])
+
+    @pl.when(step == 0)
+    def _():
+        for copy in copies():
+            copy.start()
+        for copy in copies():
+            copy.wait()
+        sum_ref[...] = jnp.zeros_like(sum_ref)
+        sum_up_ref[...] = jnp.zeros_like(sum_up_ref)
+
+    mine, theirs = mine_ref[...], theirs_ref[...]
+    mixed = join_columns(
+        [
+            dot(mine, out_w[f, 0:4].reshape(384, 256)) + dot(theirs, out_w[f, 4:8].reshape(384, 256))
+            for f in range(4)
+        ]
+    )
+    gain, last_gain = vec_ref[1:2], vec_ref[4:5]
+    z1, r1 = center(x_ref[...].astype(f32) + (mixed + vec_ref[0:1]))
+    normed = z1 * gain + vec_ref[2:3]
+    low = normed.astype(bf16)
+    nl_ref[...] = low
+    branch = vec_ref[3:4] + normed
+    for f in range(4):
+        pre = dot(low, up_w[f].reshape(D, 768)) + upb_ref[f : f + 1]
+        cdf = 0.5 + 0.5 * lax.erf(pre * (1.0 / math.sqrt(2.0)))
+        act = (pre * cdf).astype(bf16)
+        act_ref[:, f * 768 : f * 768 + 768] = act
+        slope[f] = cdf + pre * jnp.exp(-0.5 * pre * pre) * (1.0 / math.sqrt(2.0 * math.pi))
+        branch += dot(act[:, :384], down_w[2 * f].reshape(D, 384), NT)
+        branch += dot(act[:, 384:], down_w[2 * f + 1].reshape(D, 384), NT)
+    z2, r2 = center(branch)
+    y_ref[...] = (z2 * last_gain + vec_ref[5:6]).astype(bf16)
+
+    top = g_ref[...].astype(f32)
+    grad_second = norm_back(top, z2, r2, last_gain)
+    gb = grad_second.astype(bf16)
+    gb_ref[...] = gb
+    grad_normed = grad_second
+    for f in range(4):
+        ga = jnp.concatenate(
+            [dot(gb, down_w[2 * f].reshape(D, 384)), dot(gb, down_w[2 * f + 1].reshape(D, 384))], axis=1
+        )
+        gp = (ga * slope[f]).astype(bf16)
+        gp_ref[:, f * 768 : f * 768 + 768] = gp
+        sum_up_ref[f : f + 1] += jnp.sum(gp.astype(f32), axis=0, keepdims=True)
+        grad_normed += dot(gp, up_w[f].reshape(D, 768), NT)
+    grad_first = norm_back(grad_normed, z1, r1, gain)
+    gf_ref[...] = grad_first
+    gm = grad_first.astype(bf16)
+    gm32 = gm.astype(f32)
+    parts = [p.astype(bf16) for p in part_columns(gm32)]
+    gm_ref[...] = jnp.concatenate(parts, axis=1)
+    ga = sum(dot(parts[f], out_w[f].reshape(D, 256), NT) for f in range(4))
+    ga_mine_ref[...] = ga[:, :384].astype(bf16)
+    ga_theirs_ref[...] = ga[:, 384:].astype(bf16)
+
+    def total(i, value):
+        sum_ref[i : i + 1] += jnp.sum(value, axis=0, keepdims=True)
+
+    total(0, gm32)
+    total(1, grad_normed * z1)
+    total(2, grad_normed)
+    total(3, gb.astype(f32))
+    total(4, top * z2)
+    total(5, top)
+
+
+def middle(me, x, mine, theirs, g, vec, upb, up_p, down_p, out_p, block=256):
+    rows = x.shape[0]
+
+    def spec(width):
+        return pl.BlockSpec((block, width), lambda i, m: (i, 0))
+
+    def full(shape):
+        return pl.BlockSpec(shape, lambda i, m: (0, 0))
+
+    wide = [(D, bf16), (D, bf16), (FF, bf16), (D, bf16), (FF, bf16), (1024, bf16), (D, f32)]
+    wide += [(384, bf16), (384, bf16)]
+    return pl.pallas_call(
+        middle_kernel,
+        grid_spec=pltpu.PrefetchScalarGridSpec(
+            num_scalar_prefetch=1,
+            grid=(rows // block,),
+            in_specs=[spec(D), spec(384), spec(384), spec(D), full((8, D)), full((4, D))] + [ANY] * 24,
+            out_specs=[spec(w) for w, _ in wide] + [full((8, D)), full((4, D))],
+            scratch_shapes=[
+                pltpu.VMEM((4, 8, 96, 768), bf16),
+                pltpu.VMEM((8, 4, 192, 384), bf16),
+                pltpu.VMEM((4, 8, 96, 256), bf16),
+                pltpu.VMEM((4, block, 768), f32),
+                pltpu.SemaphoreType.DMA((3, 32)),
+            ],
+        ),
+        out_shape=[jax.ShapeDtypeStruct((rows, w), t) for w, t in wide]
+        + [jax.ShapeDtypeStruct((8, D), f32), jax.ShapeDtypeStruct((4, D), f32)],
+        compiler_params=params(),
+        cost_estimate=pl.CostEstimate(
+            flops=rows * (D * D + 2 * D * FF) * 8, bytes_accessed=50 * 2**20, transcendentals=rows * FF
+        ),
+        name="middle",
+    )(me, x, mine, theirs, g, vec, upb, *up_p, *down_p, *out_p)
+
+
+def grad_up_kernel(me_ref, low_ref, gp_ref, o_ref, held):
+    held[...] = dot(low_ref[...], gp_ref[...], TN).astype(bf16).reshape(8, 96, 768)
+    for rel in range(8):
+        o_ref[0, rel] = held[lax.bitwise_xor(me_ref[0], rel)]
+
+
+def grad_up(me, low, gp, dc):
+    rows = low.shape[0]
+    return pl.pallas_call(
+        grad_up_kernel,
+        grid_spec=pltpu.PrefetchScalarGridSpec(
+            num_scalar_prefetch=1,
+            grid=(2,),
+            in_specs=[
+                pl.BlockSpec((rows, D), lambda i, m: (0, 0)),
+                pl.BlockSpec(
+                    (rows, D),
+                    lambda i, m: (0, lax.bitwise_xor(m[1], i) * 2 + lax.bitwise_xor(m[2], dc)),
+                ),
+            ],
+            out_specs=pl.BlockSpec((1, 8, 96, 768), lambda i, m: (i, 0, 0, 0)),
+            scratch_shapes=[pltpu.VMEM((8, 96, 768), bf16)],
+        ),
+        out_shape=jax.ShapeDtypeStruct((2, 8, 96, 768), bf16),
+        compiler_params=params(),
+        cost_estimate=pl.CostEstimate(flops=rows * D * FF, bytes_accessed=8 * 2**20, transcendentals=0),
+        name="grad_up",
+    )(me, low, gp).reshape(2, 2, 4, 96, 768)
+
+
+def grad_down_kernel(me_ref, gb_ref, act_ref, keep_ref, send_ref, held):
+    held[...] = dot(gb_ref[...], act_ref[...], TN).astype(bf16).reshape(4, 192, 384)
+    my, mc = me_ref[1], me_ref[2]
+    for dy in range(2):
+        y2 = lax.bitwise_xor(my, dy) * 2
+        keep_ref[0, dy, 0] = held[y2 + mc]
+        send_ref[0, dy, 0] = held[y2 + 1 - mc]
+
+
+def grad_down(me, gb, act):
+    rows = gb.shape[0]
+    out = pl.BlockSpec((1, 2, 1, 192, 384), lambda i, m: (i // 4, 0, i % 4, 0, 0))
+    return pl.pallas_call(
+        grad_down_kernel,
+        grid_spec=pltpu.PrefetchScalarGridSpec(
+            num_scalar_prefetch=1,
+            grid=(8,),
+            in_specs=[
+                pl.BlockSpec((rows, D), lambda i, m: (0, 0)),
+                pl.BlockSpec((rows, 384), lambda i, m: (0, lax.bitwise_xor(m[0], i))),
+            ],
+            out_specs=[out] * 2,
+            scratch_shapes=[pltpu.VMEM((4, 192, 384), bf16)],
+        ),
+        out_shape=[jax.ShapeDtypeStruct((2, 2, 4, 192, 384), bf16)] * 2,
+        compiler_params=params(),
+        cost_estimate=pl.CostEstimate(flops=rows * D * FF * 2, bytes_accessed=13 * 2**20, transcendentals=0),
+        name="grad_down",
+    )(me, gb, act)
+
+
+def grad_out_kernel(me_ref, mine_ref, theirs_ref, gm_ref, keep_ref, send_ref, held):
+    xz, my, mc = me_ref[0], me_ref[1], me_ref[2]
+    for f in range(4):
+        gm = gm_ref[:, f * 256 : f * 256 + 256]
+        held[f, 0:4] = dot(mine_ref[...], gm, TN).astype(bf16).reshape(4, 96, 256)
+        held[f, 4:8] = dot(theirs_ref[...], gm, TN).astype(bf16).reshape(4, 96, 256)
+    for dy in range(2):
+        y2 = lax.bitwise_xor(my, dy) * 2
+        for rel in range(8):
+            at = lax.bitwise_xor(xz, rel)
+            fr = at // 2
+            pos = lax.bitwise_xor(fr % 2, mc) * 4 + lax.bitwise_xor(fr // 2, my) * 2 + at % 2
+            keep_ref[rel // 4, dy, rel % 4] = held[y2 + mc, pos]
+            send_ref[rel // 4, dy, rel % 4] = held[y2 + 1 - mc, pos]
+
+
+def grad_out(me, mine, theirs, gm):
+    rows = gm.shape[0]
+    return pl.pallas_call(
+        grad_out_kernel,
+        in_specs=[pl.BlockSpec(memory_space=pltpu.SMEM)] + [pl.BlockSpec(memory_space=pltpu.VMEM)] * 3,
+        out_specs=[pl.BlockSpec(memory_space=pltpu.VMEM)] * 2,
+        out_shape=[jax.ShapeDtypeStruct((2, 2, 4, 96, 256), bf16)] * 2,
+        scratch_shapes=[pltpu.VMEM((4, 8, 96, 256), bf16)],
+        compiler_params=params(),
+        cost_estimate=pl.CostEstimate(flops=rows * D * D * 2, bytes_accessed=6 * 2**20, transcendentals=0),
+        name="grad_out",
+    )(me, mine, theirs, gm)
+
+
+def grad_in_kernel(me_ref, x_ref, dq_ref, dk_ref, dv_ref, vec_ref, near_ref, far_ref, held):
+    xz = me_ref[0]
+    lane = lane_of((D, 128))
+    for kind, ref in enumerate((dq_ref, dk_ref, dv_ref)):
+        for dy, part in enumerate(part_columns(dot(x_ref[...], ref[...], TN))):
+            if kind == 0:
+                extra = vec_ref[...].reshape(D, 128)
+                part = jnp.concatenate([part[:, :128], jnp.where(lane < 64, part[:, 128:], extra)], axis=1)
+            held[dy] = part.astype(bf16).reshape(8, 96, 256)
+        for rel in range(8):
+            at = lax.bitwise_xor(xz, rel)
+            near_ref[rel // 4, rel % 4, kind] = held[0, at]
+            far_ref[rel // 4, rel % 4, kind] = held[1, at]
+
+
+def grad_in(me, x, dq, dk, dv, vec):
+    span = x.shape[0]
+    return pl.pallas_call(
+        grad_in_kernel,
+        in_specs=[pl.BlockSpec(memory_space=pltpu.SMEM)] + [pl.BlockSpec(memory_space=pltpu.VMEM)] * 5,
+        out_specs=[pl.BlockSpec(memory_space=pltpu.VMEM)] * 2,
+        out_shape=[jax.ShapeDtypeStruct((2, 4, 3, 96, 256), bf16)] * 2,
+        scratch_shapes=[pltpu.VMEM((2, 8, 96, 256), bf16)],
+        compiler_params=params(),
+        cost_estimate=pl.CostEstimate(flops=span * D * 2304, bytes_accessed=11 * 2**20, transcendentals=0),
+        name="grad_in",
+    )(me, x, dq, dk, dv, vec)
+
+
+def grad_token_kernel(dq_ref, dk_ref, dv_ref, w_ref, o_ref):
+    total = dot(dq_ref[...], w_ref[:, :384], NT)
+    total += dot(dk_ref[...], w_ref[:, 384:768], NT)
+    total += dot(dv_ref[...], w_ref[:, 768:], NT)
+    o_ref[...] = total.astype(o_ref.dtype)
+
+
+def grad_token(dq, dk, dv, w, part, kind, block=256):
+    count = dq.shape[0] // 2 // block
+    rows = pl.BlockSpec((block, 384), lambda i: (i + part * count, 0))
+    return pl.pallas_call(
+        grad_token_kernel,
+        grid=(count,),
+        in_specs=[rows, rows, rows, pl.BlockSpec((D, 1152), lambda i: (0, 0))],
+        out_specs=pl.BlockSpec((block, D), lambda i: (i, 0)),
+        out_shape=jax.ShapeDtypeStruct((count * block, D), kind),
+        compiler_params=params(),
+        cost_estimate=pl.CostEstimate(
+            flops=count * block * D * 2304, bytes_accessed=7 * 2**20, transcendentals=0
+        ),
+        name="grad_token",
+    )(dq, dk, dv, w)
 
 
 AXES = ("dp", "seq", "y", "c")
 SWAP = [(0, 1), (1, 0)]
 
 
-def piece_routes(pairs):
+def piece_routes():
     first, second = [], []
     for z in range(4):
-        for y in range(pairs):
+        for y in range(2):
             for c in range(2):
-                source = (z * pairs + y) * 2 + c
+                source = (z * 2 + y) * 2 + c
                 for micro in range(2):
-                    target = ((2 * micro + c) * pairs + y) * 2 + z // 2
+                    target = ((2 * micro + c) * 2 + y) * 2 + z // 2
                     (first if micro == z % 2 else second).append((source, target))
     return first, second
 
 
 def back(route):
     return [(target, source) for source, target in route]
+
+
+def along(array, axis):
+    return lax.ppermute(array, axis, SWAP)
+
+
+def across(array, step):
+    return lax.ppermute(array, "seq", [(i, i ^ step) for i in range(4)])
+
+
+def add(*arrays):
+    return sum(a.astype(f32) for a in arrays).astype(bf16)
+
+
+def column_gather(shard):
+    return jnp.stack([shard] + [across(shard, step) for step in (1, 2, 3)])
+
+
+def plane_gather(shard, order):
+    base = column_gather(shard)
+    first = along(base, order[0])
+    third, fourth = along(base, order[1]), along(first, order[1])
+    if order[0] == "y":
+        return [base, first, third, fourth]
+    return [base, third, first, fourth]
+
+
+def chip_gather(shard, order):
+    pieces = plane_gather(shard, order)
+    return pieces + [along(p, "c") for p in pieces]
+
+
+def column_reduce(pieces):
+    got = [across(pieces[step], step) for step in (1, 2, 3)]
+    return sum(a.astype(f32) for a in [pieces[0]] + got)
+
+
+def plane_reduce(near, far, order):
+    got = along(far, order[0])
+    away = along(add(near[1], got[1]), order[1])
+    return column_reduce([add(near[0][i], got[0][i], away[i]) for i in range(4)])
+
+
+def chip_reduce(keep, send, order):
+    got = along(send, "c")
+    return plane_reduce(add(keep[0], got[0]), add(keep[1], got[1]), order)
 
 
 def local_pairs(
@@ -547,13 +956,13 @@
     grad_output,
 ):
     rows = tokens.shape[2]
-    pairs = lax.axis_size("y")
-    blocks = lax.axis_size("dp") * lax.axis_size("seq")
     z = lax.axis_index("seq")
     y = lax.axis_index("y")
     c = lax.axis_index("c")
+    xz = lax.axis_index("dp") * 4 + z
+    me = jnp.stack([xz, y, c]).astype(jnp.int32)
     odd = z % 2
-    route_a, route_b = piece_routes(pairs)
+    route_a, route_b = piece_routes()
     where_to = ("seq", "y", "c")
 
     def spread(array):
@@ -570,35 +979,38 @@
             [jnp.where(odd == 0, own, other), jnp.where(odd == 0, other, own)], axis=0
         )[:, None]
 
-    def swap(array):
-        return lax.ppermute(array, "c", SWAP)
-
     vectors = (in_bias, out_bias, mid_gain, mid_shift, up_bias, down_bias, last_gain, last_shift)
+    packed = jnp.pad(jnp.concatenate(vectors).reshape(18, HEAD), ((0, 78), (0, 0)))
+    shard = in_weight.reshape(96, 3, 192).transpose(1, 0, 2)
+    extra = jnp.stack([packed, jnp.zeros_like(packed), jnp.zeros_like(packed)])
+    in_pieces = plane_gather(jnp.concatenate([shard, extra], axis=2), ("y", "dp"))
     x = spread(tokens)
-    packed = lax.all_gather(jnp.concatenate(vectors), ("dp", "seq"), axis=0, tiled=False)
+    out_pieces = chip_gather(jnp.pad(out_weight, ((0, 0), (0, 64))), ("dp", "y"))
+    up_pieces = chip_gather(up_weight, ("y", "dp"))
+    down_pieces = chip_gather(down_weight.T, ("dp", "y"))
+    g_top = spread(grad_output)
+
+    near = jnp.stack([in_pieces[0][:, 0, :18, 192:], in_pieces[2][:, 0, :18, 192:]])
+    near = near.reshape(8, 1152)
+    index = jnp.arange(8, dtype=jnp.int32) ^ xz
+    known = jnp.dot(
+        (index[:, None] == jnp.arange(8, dtype=jnp.int32)[None, :]).astype(bf16),
+        near,
+        preferred_element_type=f32,
+    )
     whole = []
     at = 0
     for v in vectors:
-        whole.append(packed[:, at : at + v.shape[0]].reshape(-1).astype(f32))
+        whole.append(known[:, at : at + v.shape[0]].reshape(-1))
         at += v.shape[0]
     in_vector, out_vector, mid_scale, mid_offset, up_vector, down_vector, last_scale, last_offset = whole
-
-    w_in = lax.all_gather(in_weight, ("dp", "seq", "y"), axis=0, tiled=False)
-    w_in = w_in.reshape(blocks, pairs, D // blocks, 3, 3, HEAD)
-    n = pairs * 3
-
-    def columns(weight):
-        full = lax.all_gather(weight, AXES, axis=0, tiled=False)
-        full = full.reshape(blocks, 2 * pairs, weight.shape[0], weight.shape[1])
-        return full.transpose(0, 2, 1, 3).reshape(blocks * weight.shape[0], -1)
-
-    w_out = columns(out_weight)
-    w_up = columns(up_weight)
-    w_down = columns(down_weight)
-    g_top = spread(grad_output)
+    zero = jnp.zeros_like(out_vector)
+    vec = jnp.stack(
+        [out_vector, mid_scale, mid_offset, down_vector, last_scale, last_offset, zero, zero]
+    )
 
     micro = z // 2
-    group = (lax.axis_index("dp") * pairs + y) * 2 + odd
+    group = (lax.axis_index("dp") * 2 + y) * 2 + odd
     length = lengths[micro, group]
     iota = jnp.arange(rows, dtype=jnp.int32)
 
@@ -607,110 +1019,54 @@
 
     place = jnp.concatenate(places(c) + places(1 - c))
     mask = jnp.where(place < length, 0.0, -1e30).astype(bf16)
-    span = 4 * rows
     half = 2 * rows
     lane = jnp.arange(128, dtype=jnp.int32)[None, :]
     aux = jnp.where(
         lane == 64, mask[:, None], jnp.where((lane > 64) & (lane < 68), -1.0, 0.0).astype(bf16)
     )
 
-    x_full = jnp.concatenate([x, swap(x)], axis=0)
-    w_head = jnp.pad(
-        w_in.transpose(1, 3, 0, 2, 4, 5).reshape(n, D, 192), ((0, 0), (0, 0), (0, 64))
-    )
-    bias = lax.dynamic_index_in_dim(
-        in_vector.reshape(pairs, 2, 3, 2, HEAD), c, 1, keepdims=False
-    ).reshape(n, 2, HEAD)
+    def by_distance(array):
+        return jnp.where(y == 0, array, array[::-1])
+
+    x_full = jnp.concatenate([x, along(x, "c")], axis=0)
+    bias = lax.dynamic_index_in_dim(in_vector.reshape(2, 2, 3, 2, HEAD), c, 1, keepdims=False)
+    bias = by_distance(bias).reshape(6, 2, HEAD)
     b_head = jnp.concatenate(
         [bias[:, 0], jnp.zeros_like(bias[:, 0]), bias[:, 1], jnp.zeros_like(bias[:, 0])], axis=1
     )[:, None]
-    q, k, v = project(x_full, w_head, b_head, aux)
+    q, k, v, w_kind = project(me, x_full, b_head, aux, in_pieces)
     attended, q = attend(q, k, v)
     mine = attended[:half]
-    theirs = swap(attended[half:])
-
-    def by_core(own, other):
-        even = jnp.where(c == 0, own, other).reshape(half, pairs, 1, 192)
-        odd_ = jnp.where(c == 0, other, own).reshape(half, pairs, 1, 192)
-        return jnp.concatenate([even, odd_], axis=2).reshape(half, D)
-
-    att = by_core(mine, theirs)
-    mixed = dot(att, w_out) + out_vector
-    first_std, first_scale = standardize(x.astype(f32) + mixed)
-    normed = first_std * mid_scale + mid_offset
-    normed_low = normed.astype(bf16)
-    pre_up = dot(normed_low, w_up) + up_vector
-    act_low = jax.nn.gelu(pre_up, approximate=False).astype(bf16)
-    branch = dot(act_low, w_down) + down_vector
-    second_std, second_scale = standardize(normed + branch)
-    result = collect((second_std * last_scale + last_offset).astype(bf16))
-
-    g_top = g_top.astype(f32)
-    vec_last_gain = jnp.sum(g_top * second_std, axis=0)
-    vec_last_shift = jnp.sum(g_top, axis=0)
-    grad_second = norm_back(g_top, second_std, second_scale, last_scale)
-    grad_branch = grad_second.astype(bf16)
-    vec_down = row_sum(grad_branch)
-    grad_down = dot(act_low, grad_branch, TN)
-    grad_pre = (dot(grad_branch, w_down, NT) * gelu_slope(pre_up)).astype(bf16)
-    vec_up = row_sum(grad_pre)
-    grad_up = dot(normed_low, grad_pre, TN)
-    grad_normed = grad_second + dot(grad_pre, w_up, NT)
-    vec_mid_gain = jnp.sum(grad_normed * first_std, axis=0)
-    vec_mid_shift = jnp.sum(grad_normed, axis=0)
-    grad_first = norm_back(grad_normed, first_std, first_scale, mid_scale)
-    grad_mixed = grad_first.astype(bf16)
-    vec_out = row_sum(grad_mixed)
-    grad_out = dot(att, grad_mixed, TN)
-    grad_att = dot(grad_mixed, w_out, NT).astype(bf16).reshape(half, pairs, 2, 192)
-    g_even = grad_att[:, :, 0].reshape(half, n * HEAD)
-    g_odd = grad_att[:, :, 1].reshape(half, n * HEAD)
-    g_own = jnp.where(c == 0, g_even, g_odd)
-    g_other = swap(jnp.where(c == 0, g_odd, g_even))
+    theirs = along(attended[half:], "c")
+    (result, low, act, gb, gp, gm, grad_first, g_own, g_other, sums, sums_up) = middle(
+        me, x, mine, theirs, g_top, vec, up_vector.reshape(4, D), up_pieces, down_pieces, out_pieces
+    )
+    result = collect(result)
+
+    g_other = along(g_other, "c")
+    up_send = grad_up(me, low, gp, 1)
+    up_keep = grad_up(me, low, gp, 0)
+    down_keep, down_send = grad_down(me, gb, act)
+    out_keep, out_send = grad_out(me, mine, theirs, gm)
     dq, dk, dv = attend_back(q, k, v, attended, jnp.concatenate([g_own, g_other], axis=0))
-
-    def scatter(grad, weight):
-        r, w = weight.shape
-        grad = grad.astype(bf16).reshape(blocks, r, 2 * pairs, w).transpose(0, 2, 1, 3)
-        return lax.psum_scatter(
-            grad.reshape(2 * pairs * blocks, r, w), AXES, scatter_dimension=0, tiled=True
-        )[0].astype(f32)
-
-    out_down = scatter(grad_down, down_weight)
-    out_up = scatter(grad_up, up_weight)
-    out_out = scatter(grad_out, out_weight)
-    grad_proj = jnp.concatenate([dq, dk, dv], axis=1)
-    grad_in = dot(x_full, grad_proj, TN).astype(bf16)
-    r = in_weight.shape[0]
-    grad_in = grad_in.reshape(blocks, r, 3, pairs, 192).transpose(0, 3, 1, 2, 4)
-    out_in = lax.psum_scatter(
-        grad_in.reshape(blocks * pairs, r, 576), ("dp", "seq", "y"), scatter_dimension=0, tiled=True
-    )[0]
-    out_in = out_in.reshape(r, 3, 3, HEAD).transpose(0, 2, 1, 3).reshape(r, 576).astype(f32)
-    w_kind = w_in.transpose(0, 2, 4, 1, 3, 5).reshape(D, 3 * n * HEAD)
-    grad_x = dot(grad_proj, w_kind, NT)
-    grad_x = grad_first + grad_x[:half] + swap(grad_x[half:].astype(bf16)).astype(f32)
-    grad_tokens = collect(grad_x.astype(bf16)).astype(f32)
-    own_bias = jnp.stack(
-        [row_sum(dq).reshape(pairs, 3, HEAD), row_sum(dv).reshape(pairs, 3, HEAD)], axis=2
-    )
+    out_up = chip_reduce(up_keep, up_send, ("y", "dp"))
+    out_down = chip_reduce(down_keep, down_send, ("dp", "y")).T
+    out_out = chip_reduce(out_keep, out_send, ("dp", "y"))[:, :192]
+
     core = (jnp.arange(2) == c).astype(f32)
-    vec_in = (own_bias[:, None] * core[None, :, None, None, None]).reshape(-1)
-    grads = (
-        vec_in,
-        vec_out,
-        vec_mid_gain,
-        vec_mid_shift,
-        vec_up,
-        vec_down,
-        vec_last_gain,
-        vec_last_shift,
-    )
-    packed = jnp.concatenate([g.reshape(blocks, -1) for g in grads], axis=1)
-    total = lax.psum(packed, AXES)
-    total = lax.dynamic_index_in_dim(
-        total, lax.axis_index("dp") * lax.axis_size("seq") + z, 0, keepdims=False
-    )
+    own_bias = jnp.stack([row_sum(dq).reshape(2, 3, HEAD), row_sum(dv).reshape(2, 3, HEAD)], axis=2)
+    vec_in = (by_distance(own_bias)[:, None] * core[None, :, None, None, None]).reshape(-1)
+    grads = (vec_in, sums[0], sums[1], sums[2], sums_up, sums[3], sums[4], sums[5])
+    packed = jnp.concatenate([g.reshape(8, -1) for g in grads], axis=1).reshape(8, 18, HEAD)
+    packed = jnp.pad(packed, ((0, 0), (0, 78), (64, 0)))
+    in_near, in_far = grad_in(me, x_full, dq, dk, dv, packed)
+    partial = along(grad_token(dq, dk, dv, w_kind, 1, bf16), "c")
+    got = plane_reduce(in_near, in_far, ("y", "dp"))
+    out_in = got[:, :, :192].reshape(3, 96, 3, HEAD).transpose(1, 2, 0, 3).reshape(96, 576)
+    total = got[0, :18, 192:].reshape(1152)
+    total = total + along(total, "c")
+    own = grad_token(dq, dk, dv, w_kind, 0, f32)
+    grad_tokens = collect((grad_first + own + partial.astype(f32)).astype(bf16)).astype(f32)
     sums = []
     at = 0
     for vector in vectors:
@@ -746,9 +1102,8 @@
 
 
 def solution(mesh):
-    dp, seq, fsdp = (mesh.shape[name] for name in ("dp", "seq", "fsdp"))
-    if seq == 2 * MICRO and fsdp % 2 == 0:
-        mesh = jax.sharding.Mesh(mesh.devices.reshape(dp, seq, fsdp // 2, 2), AXES)
+    if tuple(mesh.shape[name] for name in ("dp", "seq", "fsdp")) == (2, 4, 4):
+        mesh = jax.sharding.Mesh(mesh.devices.reshape(2, 4, 2, 2), AXES)
         body, (ins, outs) = local_pairs, specs(("y", "c"))
     else:
         body, (ins, outs) = local, specs(("fsdp",))

time: 862 us -> 563 us (0.65)
  waiting for transfers between devices: 273 us -> 141 us
  blocking collectives: 120 us -> 0 us
  Pallas kernels: 138 us -> 242 us
  local copies, waits for them, and re-layouts: 146 us -> 43 us
  matrix products: 100 us -> 0.19 us
  starting transfers between devices: 25.2 us -> 79.9 us
  between operations: 15 us -> 1.68 us
  other arithmetic: 33.8 us -> 44 us
    reduce_scatter x4 -> x0, waiting for transfers between devices: 174 us -> none  [the longest x3 174 us: scatter(): lax.psum_scatter(grad.reshape(2 * pairs * blocks, r, w), AXES, scatter_di...]
    ppermute x4 -> x64, waiting for transfers between devices: 0.49 us -> 118 us  [the longest x24 67.8 us: across(): return lax.ppermute(array, 'seq', [(i, i ^ step) for i in range(4)])]
    pallas_call x1 -> x9, Pallas kernels: 10.2 us -> 115 us  [the longest x1 46.6 us: middle(): pl.pallas_call(middle_kernel, grid_spec=pltpu.PrefetchScalarGridSpec(num_...]
    dot_general x11 -> x1, matrix products: 100 us -> 0.19 us  [local_pairs(): jnp.dot((index[:, None] == jnp.arange(8, dtype=jnp.int32)[None, :]).astyp...]
    reshape x20 -> x5, local copies, waits for them, and re-layouts: 77 us -> 0.42 us  [the longest x1 0.14 us: local_pairs(): shard = in_weight.reshape(96, 3, 192).transpose(1, 0, 2)]
    all_gather x1 -> x0, blocking collectives: 66.2 us -> none  [local_pairs(): lax.all_gather(jnp.concatenate(vectors), ('dp', 'seq'), axis=0, tiled=False)]
    all_gather x4 -> x0, waiting for transfers between devices: 64.5 us -> none  [the longest x3 64.5 us: columns(): full = lax.all_gather(weight, AXES, axis=0, tiled=False)]
    psum x1 -> x0, blocking collectives: 53.5 us -> none  [local_pairs(): total = lax.psum(packed, AXES)]
  transfers between devices with their start and end apart: 20 -> 72, of which waited for: 6 -> 20; matrix products, arithmetic and copies ran while one was open for 28% -> 14% of each run, Pallas kernels for 16% -> 34%
where the time goes in v2:
time: 563 us; the launch traced here: 552 us
  Pallas kernels  242 us (43%)
  waiting for transfers between devices  141 us (25%)
  starting transfers between devices  79.9 us (14%)
  other arithmetic  44 us (8%)
  local copies, waits for them, and re-layouts  43 us (8%)
    pallas_call x1, Pallas kernels, attend_back(): pl.pallas_call(attend_back_kernel, grid=(n // 2, span // block), in_specs...  79.6 us
    ppermute x24, waiting for transfers between devices, across(): return lax.ppermute(array, 'seq', [(i, i ^ step) for i in range(4)])  67.8 us
    ppermute x40, waiting for transfers between devices, along(): return lax.ppermute(array, axis, SWAP)  50.2 us
    pallas_call x1, Pallas kernels, attend(): pl.pallas_call(attend_kernel, grid=(n // 2, span // block), in_specs=[par...  47.9 us
    pallas_call x1, Pallas kernels, middle(): pl.pallas_call(middle_kernel, grid_spec=pltpu.PrefetchScalarGridSpec(num_...  46.6 us
    ppermute x40, starting transfers between devices, along(): return lax.ppermute(array, axis, SWAP)  27.5 us
    ppermute x24, starting transfers between devices, across(): return lax.ppermute(array, 'seq', [(i, i ^ step) for i in range(4)])  24.5 us
    ppermute x2, waiting for transfers between devices, collect(): other = lax.ppermute(array[rows:], where_to, back(route_b))  23.3 us
  transfers between devices with their start and end apart: 72, of which 20 were waited for; matrix products, arithmetic and copies ran while one was open for 14% of the time, Pallas kernels for 34%

profile of v2, /device:TPU:0, one launch (start us, length us, event | category | flops | bytes accessed | tf_op | source)
XLA Modules:
  0.0 552.3 jit_solution(4931028300018153885)
XLA Ops:
  2.1 4.0 collective-permute-start.33
  7.7 5.4 concatenate.41
  19.8 7.4 %collective-permute-start = (bf16[512,768]{1,0:T(8,128)(2,1)}, bf16[512,768]{1,0:T(8,128)(2,1)}, u32[]{:S(2)}, u32[]{:S(2)}) collective-permute-start(bf16[512,768]{1,0:T(8,128)(2,1)} %get-tuple-element.130), channel_id=1, source_target_pairs={{0,0},{1,4},{2,2},{3,6},{4,8},{5,12},{6,10},{7,14},{8,1},{9,5},{10... | collective-permute-start | bytes 2359304 | tf_op jit(solution)/shard_map/ppermute | solution.py:972
  30.6 3.4 collective-permute-start.1
  36.1 3.1 collective-permute-done.3
  44.3 29.5 %collective-permute-done.23 = bf16[192,384]{1,0:T(8,128)(2,1)S(1)} collective-permute-done((bf16[192,384]{1,0:T(8,128)(2,1)}, bf16[192,384]{1,0:T(8,128)(2,1)S(1)}, u32[]{:S(2)}, u32[]{:S(2)}) %collective-permute-start.23) | collective-permute-done | bytes 147488 | tf_op jit(solution)/shard_map/ppermute | solution.py:900
  89.2 3.5 collective-permute-done.13
  98.8 15.1 %collective-permute-done.37.rest_19_ = bf16[4,96,256]{2,1,0:T(8,128)(2,1)} collective-permute-done((bf16[4,96,256]{2,1,0:T(8,128)(2,1)}, bf16[4,96,256]{2,1,0:T(8,128)(2,1)}, u32[]{:S(2)}, u32[]{:S(2)}) %collective-permute-start.37) | collective-permute-done | bytes 196640 | tf_op jit(solution)/shard_map/ppermute | solution.py:896
  121.3 8.6 %collective-permute-done.8.rest_3_ = bf16[4,3,96,256]{3,2,1,0:T(8,128)(2,1)S(1)} collective-permute-done((bf16[4,3,96,256]{3,2,1,0:T(8,128)(2,1)}, bf16[4,3,96,256]{3,2,1,0:T(8,128)(2,1)S(1)}, u32[]{:S(2)}, u32[]{:S(2)}) %collective-permute-start.8) | collective-permute-done | bytes 589856 | tf_op jit(solution)/shard_map/ppermute | solution.py:896
  133.4 13.6 %project.1 = (bf16[6,2048,128]{2,1,0:T(8,128)(2,1)}, bf16[6,2048,128]{2,1,0:T(8,128)(2,1)}, bf16[6,2048,128]{2,1,0:T(8,128)(2,1)}, bf16[768,1152]{1,0:T(8,128)(2,1)}) custom-call(s32[3]{0:T(128)} %pad_add_fusion.me_ref, bf16[2048,768]{1,0:T(8,128)(2,1)} %constant_dynamic-update-slice_fusion.2.x_ref, f32[6,1,256]{2,1,0:T(1,128)} %broadcast_in_dim.53.b_ref, ...), custom_call_target="tpu_custom_call" | custom-call | flops 4831838208 | bytes 9437184 | tf_op jit(solution)/shard_map/project/pallas_call | solution.py:559
  151.7 47.9 %attend.1 = (bf16[2048,384]{1,0:T(8,128)(2,1)}, bf16[6,2048,128]{2,1,0:T(8,128)(2,1)}) custom-call(bf16[6,2048,128]{2,1,0:T(8,128)(2,1)} %get-tuple-element.40.q_ref, bf16[6,2048,128]{2,1,0:T(8,128)(2,1)} %get-tuple-element.41.k_ref, bf16[6,2048,128]{2,1,0:T(8,128)(2,1)} %get-tuple-element.42.v_ref), custom_call_target="tpu_custom_call" | custom-call | flops 12884901888 | bytes 12582912 | tf_op jit(solution)/shard_map/attend/pallas_call | solution.py:62
  208.4 46.6 %middle.1 = (bf16[1024,768]{1,0:T(8,128)(2,1)}, bf16[1024,768]{1,0:T(8,128)(2,1)}, bf16[1024,3072]{1,0:T(8,128)(2,1)}, bf16[1024,768]{1,0:T(8,128)(2,1)}, bf16[1...) custom-call(s32[3]{0:T(128)} %pad_add_fusion.me_ref, ...), custom_call_target="tpu_custom_call" | custom-call | flops 43486543872 | bytes 52428800 | tf_op jit(solution)/shard_map/middle/pallas_call | solution.py:706
  257.8 5.2 grad_out.1
  263.1 7.4 %collective-permute-start.42 = (bf16[512,768]{1,0:T(8,128)(2,1)}, bf16[512,768]{1,0:T(8,128)(2,1)}, u32[]{:S(2)}, u32[]{:S(2)}) collective-permute-start(bf16[512,768]{1,0:T(8,128)(2,1)} %get-tuple-element.123), channel_id=1, source_target_pairs={{0,0},{4,1},{2,2},{6,3},{8,4},{12,5},{10,6},{14,7},{1,8},{5,9},{3,... | collective-permute-start | bytes 2359304 | tf_op jit(solution)/shard_map/ppermute | solution.py:976
  270.5 6.9 %grad_up.2 = bf16[2,8,96,768]{3,2,1,0:T(8,128)(2,1)} custom-call(s32[3]{0:T(128)} %pad_add_fusion.me_ref, bf16[1024,768]{1,0:T(8,128)(2,1)} %get-tuple-element.60.low_ref, bf16[1024,3072]{1,0:T(8,128)(2,1)} %get-tuple-element.61.gp_ref), custom_call_target="tpu_custom_call" | custom-call | flops 2415919104 | bytes 8388608 | tf_op jit(solution)/shard_map/grad_up/pallas_call | solution.py:739
  280.3 6.8 %grad_up.3 = bf16[2,8,96,768]{3,2,1,0:T(8,128)(2,1)} custom-call(s32[3]{0:T(128)} %pad_add_fusion.me_ref, bf16[1024,768]{1,0:T(8,128)(2,1)} %get-tuple-element.60.low_ref, bf16[1024,3072]{1,0:T(8,128)(2,1)} %get-tuple-element.61.gp_ref), custom_call_target="tpu_custom_call" | custom-call | flops 2415919104 | bytes 8388608 | tf_op jit(solution)/shard_map/grad_up/pallas_call | solution.py:739
  291.1 12.9 %grad_down.1 = (bf16[2,2,4,192,384]{4,3,2,1,0:T(8,128)(2,1)}, bf16[2,2,4,192,384]{4,3,2,1,0:T(8,128)(2,1)}) custom-call(s32[3]{0:T(128)} %pad_add_fusion.me_ref, bf16[1024,768]{1,0:T(8,128)(2,1)} %get-tuple-element.62.gb_ref, bf16[1024,3072]{1,0:T(8,128)(2,1)} %get-tuple-element.63.act_ref), custom_call_target="tpu_custom_call" | custom-call | flops 4831838208 | bytes 13631488 | tf_op jit(solution)/shard_map/grad_down/pallas_call | solution.py:773
  306.5 79.6 %attend_back.1 = (bf16[2048,384]{1,0:T(8,128)(2,1)}, bf16[2048,384]{1,0:T(8,128)(2,1)}, bf16[2048,384]{1,0:T(8,128)(2,1)}) custom-call(bf16[6,2048,128]{2,1,0:T(8,128)(2,1)} %get-tuple-element.46.q_ref, bf16[6,2048,128]{2,1,0:T(8,128)(2,1)} %get-tuple-element.41.k_ref, bf16[6,2048,128]{2,1,0:T(8,128)(2,1)} %get-tuple-element.42.v_ref, ...), custom_call_target="tpu_custom_call" | custom-call | flops 32212254720 | bytes 12582912 | tf_op jit(solution)/shard_map/attend_back/pallas_call | solution.py:126
  394.8 9.9 %grad_in.1 = (bf16[2,4,3,96,256]{4,3,2,1,0:T(8,128)(2,1)}, bf16[2,4,3,96,256]{4,3,2,1,0:T(8,128)(2,1)}) custom-call(s32[3]{0:T(128)} %pad_add_fusion.me_ref, bf16[2048,768]{1,0:T(8,128)(2,1)} %constant_dynamic-update-slice_fusion.2.x_ref, bf16[2048,384]{1,0:T(8,128)(2,1)} %get-tuple-element.49.dq_ref, bf16[2048,384]{1,0:T(8,128)(2,1)} %get-tuple-element.50.dk_ref, ...), custom_call_target="tpu_custom_call" | custom-call | flops 3623878656 | bytes 11534336 | tf_op jit(solution)/shard_map/grad_in/pallas_call | solution.py:839
  404.7 6.3 %grad_token.3 = bf16[1024,768]{1,0:T(8,128)(2,1)} custom-call(bf16[2048,384]{1,0:T(8,128)(2,1)} %get-tuple-element.49.dq_ref, bf16[2048,384]{1,0:T(8,128)(2,1)} %get-tuple-element.50.dk_ref, bf16[2048,384]{1,0:T(8,128)(2,1)} %get-tuple-element.51.dv_ref, bf16[768,1152]{1,0:T(8,128)(2,1)} %get-tuple-element.52.w_ref), custom_call_target="tpu_custom_call" | custom-call | flops 1811939328 | bytes 7340032 | tf_op jit(solution)/shard_map/grad_token/pallas_call | solution.py:861
  415.4 6.6 %grad_token.2 = f32[1024,768]{1,0:T(8,128)} custom-call(bf16[2048,384]{1,0:T(8,128)(2,1)} %get-tuple-element.49.dq_ref, bf16[2048,384]{1,0:T(8,128)(2,1)} %get-tuple-element.50.dk_ref, bf16[2048,384]{1,0:T(8,128)(2,1)} %get-tuple-element.51.dv_ref, bf16[768,1152]{1,0:T(8,128)(2,1)} %get-tuple-element.52.w_ref), custom_call_target="tpu_custom_call" | custom-call | flops 1811939328 | bytes 7340032 | tf_op jit(solution)/shard_map/grad_token/pallas_call | solution.py:861
  425.1 18.3 %collective-permute-done.56 = bf16[4,96,256]{2,1,0:T(8,128)(2,1)S(1)} collective-permute-done((bf16[4,96,256]{2,1,0:T(8,128)(2,1)S(1)}, bf16[4,96,256]{2,1,0:T(8,128)(2,1)S(1)}, u32[]{:S(2)}, u32[]{:S(2)}) %collective-permute-start.56) | collective-permute-done | bytes 196640 | tf_op jit(solution)/shard_map/ppermute | solution.py:896
  447.1 3.5 fusion.1
  452.1 3.5 add_convert_fusion.2
  457.0 5.1 collective-permute-done.49
  462.8 4.0 collective-permute-start.52
  470.1 3.2 collective-permute-done.52
  474.7 3.8 collective-permute-done.51
  478.7 7.4 %collective-permute-start.46 = (bf16[512,768]{1,0:T(8,128)(2,1)}, bf16[512,768]{1,0:T(8,128)(2,1)}, u32[]{:S(2)}, u32[]{:S(2)}) collective-permute-start(bf16[512,768]{1,0:T(8,128)(2,1)} %get-tuple-element.119), channel_id=1, source_target_pairs={{0,0},{4,1},{2,2},{6,3},{8,4},{12,5},{10,6},{14,7},{1,8},{5,9},{3,... | collective-permute-start | bytes 2359304 | tf_op jit(solution)/shard_map/ppermute | solution.py:976
  495.0 23.3 %collective-permute-done.47 = bf16[512,768]{1,0:T(8,128)(2,1)} collective-permute-done((bf16[512,768]{1,0:T(8,128)(2,1)}, bf16[512,768]{1,0:T(8,128)(2,1)}, u32[]{:S(2)}, u32[]{:S(2)}) %collective-permute-start.47) | collective-permute-done | bytes 786464 | tf_op jit(solution)/shard_map/ppermute | solution.py:977
  529.7 3.9 collective-permute-done.63
  533.6 12.5 %collective-permute-done.64 = bf16[96,768]{1,0:T(8,128)(2,1)S(1)} collective-permute-done((bf16[96,768]{1,0:T(8,128)(2,1)S(1)}, bf16[96,768]{1,0:T(8,128)(2,1)S(1)}, u32[]{:S(2)}, u32[]{:S(2)}) %collective-permute-start.64) | collective-permute-done | bytes 147488 | tf_op jit(solution)/shard_map/ppermute | solution.py:900
  (305 shorter events, 132.5 us)
Async XLA Ops:
  2.1 28.3 %collective-permute-start.33 = (bf16[96,256]{1,0:T(8,128)(2,1)}, bf16[96,256]{1,0:T(8,128)(2,1)S(1)}, u32[]{:S(2)}, u32[]{:S(2)}) collective-permute-start(bf16[96,256]{1,0:T(8,128)(2,1)} %get-tuple-element.139), channel_id=1, source_target_pairs={{0,8},{4,12},{8,0},{12,4},{1,9},{5,13},{9,1},{13,5},{2,10},{6,14},... | collective-permute-start | bytes 147464 | tf_op jit(solution)/shard_map/ppermute | solution.py:900
  6.1 24.3 %collective-permute-start.32 = (bf16[96,256]{1,0:T(8,128)(2,1)}, bf16[96,256]{1,0:T(8,128)(2,1)}, u32[]{:S(2)}, u32[]{:S(2)}) collective-permute-start(bf16[96,256]{1,0:T(8,128)(2,1)} %get-tuple-element.139), channel_id=1, source_target_pairs={{0,4},{4,0},{8,12},{12,8},{1,5},{5,1},{9,13},{13,9},{2,6},{6,2},{1... | collective-permute-start | bytes 147464 | tf_op jit(solution)/shard_map/ppermute | solution.py:900
  7.7 22.9 %collective-permute-start.34 = (bf16[96,256]{1,0:T(8,128)(2,1)}, bf16[96,256]{1,0:T(8,128)(2,1)}, u32[]{:S(2)}, u32[]{:S(2)}) collective-permute-start(bf16[96,256]{1,0:T(8,128)(2,1)} %get-tuple-element.139), channel_id=1, source_target_pairs={{0,12},{4,8},{8,4},{12,0},{1,13},{5,9},{9,5},{13,1},{2,14},{6,10},... | collective-permute-start | bytes 147464 | tf_op jit(solution)/shard_map/ppermute | solution.py:900
  19.8 62.3 %collective-permute-start = (bf16[512,768]{1,0:T(8,128)(2,1)}, bf16[512,768]{1,0:T(8,128)(2,1)}, u32[]{:S(2)}, u32[]{:S(2)}) collective-permute-start(bf16[512,768]{1,0:T(8,128)(2,1)} %get-tuple-element.130), channel_id=1, source_target_pairs={{0,0},{1,4},{2,2},{3,6},{4,8},{5,12},{6,10},{7,14},{8,1},{9,5},{10... | collective-permute-start | bytes 2359304 | tf_op jit(solution)/shard_map/ppermute | solution.py:972
  30.6 54.1 %collective-permute-start.1 = (bf16[512,768]{1,0:T(8,128)(2,1)}, bf16[512,768]{1,0:T(8,128)(2,1)S(1)}, u32[]{:S(2)}, u32[]{:S(2)}) collective-permute-start(bf16[512,768]{1,0:T(8,128)(2,1)} %get-tuple-element.129), channel_id=1, source_target_pairs={{0,8},{1,12},{2,10},{3,14},{4,0},{5,4},{6,2},{7,6},{8,9},{9,13},{1... | collective-permute-start | bytes 2359304 | tf_op jit(solution)/shard_map/ppermute | solution.py:972
  34.5 39.3 %collective-permute-start.23 = (bf16[192,384]{1,0:T(8,128)(2,1)}, bf16[192,384]{1,0:T(8,128)(2,1)S(1)}, u32[]{:S(2)}, u32[]{:S(2)}) collective-permute-start(bf16[192,384]{1,0:T(8,128)(2,1)} %bitcast.25), channel_id=1, source_target_pairs={{0,8},{4,12},{8,0},{12,4},{1,9},{5,13},{9,1},{13,5},{2,10},{6,14},... | collective-permute-start | bytes 442376 | tf_op jit(solution)/shard_map/ppermute | solution.py:900
  39.2 37.0 %collective-permute-start.22 = (bf16[192,384]{1,0:T(8,128)(2,1)}, bf16[192,384]{1,0:T(8,128)(2,1)S(1)}, u32[]{:S(2)}, u32[]{:S(2)}) collective-permute-start(bf16[192,384]{1,0:T(8,128)(2,1)} %bitcast.25), channel_id=1, source_target_pairs={{0,4},{4,0},{8,12},{12,8},{1,5},{5,1},{9,13},{13,9},{2,6},{6,2},{1... | collective-permute-start | bytes 442376 | tf_op jit(solution)/shard_map/ppermute | solution.py:900
  41.5 36.9 %collective-permute-start.24 = (bf16[192,384]{1,0:T(8,128)(2,1)}, bf16[192,384]{1,0:T(8,128)(2,1)S(1)}, u32[]{:S(2)}, u32[]{:S(2)}) collective-permute-start(bf16[192,384]{1,0:T(8,128)(2,1)} %bitcast.25), channel_id=1, source_target_pairs={{0,12},{4,8},{8,4},{12,0},{1,13},{5,9},{9,5},{13,1},{2,14},{6,10},... | collective-permute-start | bytes 442376 | tf_op jit(solution)/shard_map/ppermute | solution.py:900
  92.7 37.8 %collective-permute-start.2 = (bf16[1024,768]{1,0:T(8,128)(2,1)}, bf16[1024,768]{1,0:T(8,128)(2,1)S(1)}, u32[]{:S(2)}, u32[]{:S(2)}) collective-permute-start(bf16[1024,768]{1,0:T(8,128)(2,1)} %get-tuple-element.135.x_ref), channel_id=1, source_target_pairs={{0,1},{1,0},{2,3},{3,2},{4,5},{5,4},{6,7},{7,6},{8,9},{9,8},{10,11... | collective-permute-start | bytes 4718600 | tf_op jit(solution)/shard_map/ppermute | solution.py:896
  97.2 23.0 %collective-permute-start.16 = (bf16[4,96,768]{2,1,0:T(8,128)(2,1)}, bf16[4,96,768]{2,1,0:T(8,128)(2,1)S(1)}, u32[]{:S(2)}, u32[]{:S(2)}) collective-permute-start(bf16[4,96,768]{2,1,0:T(8,128)(2,1)} %pad_maximum_fusion.3.rest_0_), channel_id=1, source_target_pairs={{0,16},{16,0},{1,17},{17,1},{2,18},{18,2},{3,19},{19,3},{4,20},{20... | collective-permute-start | bytes 1769480 | tf_op jit(solution)/shard_map/ppermute | solution.py:896
  117.2 33.9 %collective-permute-start.10 = (bf16[512,768]{1,0:T(8,128)(2,1)S(1)}, bf16[512,768]{1,0:T(8,128)(2,1)S(1)}, u32[]{:S(2)}, u32[]{:S(2)}) collective-permute-start(bf16[512,768]{1,0:T(8,128)(2,1)S(1)} %get-tuple-element.125), channel_id=1, source_target_pairs={{0,0},{1,4},{2,2},{3,6},{4,8},{5,12},{6,10},{7,14},{8,1},{9,5},{10... | collective-permute-start | bytes 2359304 | tf_op jit(solution)/shard_map/ppermute | solution.py:972
  118.6 28.4 %collective-permute-start.15 = (bf16[4,96,768]{2,1,0:T(8,128)(2,1)}, bf16[4,96,768]{2,1,0:T(8,128)(2,1)S(1)}, u32[]{:S(2)}, u32[]{:S(2)}) collective-permute-start(bf16[4,96,768]{2,1,0:T(8,128)(2,1)} %pad_maximum_fusion.3.rest_0_), channel_id=1, source_target_pairs={{0,2},{2,0},{1,3},{3,1},{4,6},{6,4},{5,7},{7,5},{8,10},{10,8},{9,1... | collective-permute-start | bytes 1769480 | tf_op jit(solution)/shard_map/ppermute | solution.py:896
  120.2 28.4 %collective-permute-start.28 = (bf16[4,192,384]{2,1,0:T(8,128)(2,1)}, bf16[4,192,384]{2,1,0:T(8,128)(2,1)}, u32[]{:S(2)}, u32[]{:S(2)}) collective-permute-start(bf16[4,192,384]{2,1,0:T(8,128)(2,1)} %pad_maximum_fusion.4.rest_8_), channel_id=1, source_target_pairs={{0,1},{1,0},{2,3},{3,2},{4,5},{5,4},{6,7},{7,6},{8,9},{9,8},{10,11... | collective-permute-start | bytes 1769480 | tf_op jit(solution)/shard_map/ppermute | solution.py:896
  147.0 55.0 %collective-permute-start.11 = (bf16[512,768]{1,0:T(8,128)(2,1)S(1)}, bf16[512,768]{1,0:T(8,128)(2,1)S(1)}, u32[]{:S(2)}, u32[]{:S(2)}) collective-permute-start(bf16[512,768]{1,0:T(8,128)(2,1)S(1)} %get-tuple-element.126), channel_id=1, source_target_pairs={{0,8},{1,12},{2,10},{3,14},{4,0},{5,4},{6,2},{7,6},{8,9},{9,13},{1... | collective-permute-start | bytes 2359304 | tf_op jit(solution)/shard_map/ppermute | solution.py:972
  148.6 54.0 %collective-permute-start.19 = (bf16[4,96,768]{2,1,0:T(8,128)(2,1)S(1)}, bf16[4,96,768]{2,1,0:T(8,128)(2,1)S(1)}, u32[]{:S(2)}, u32[]{:S(2)}) collective-permute-start(bf16[4,96,768]{2,1,0:T(8,128)(2,1)S(1)} %collective-permute-done.15.rest_1_), channel_id=1, source_target_pairs={{0,1},{1,0},{2,3},{3,2},{4,5},{5,4},{6,7},{7,6},{8,9},{9,8},{10,11... | collective-permute-start | bytes 1769480 | tf_op jit(solution)/shard_map/ppermute | solution.py:896
  149.9 52.9 %collective-permute-start.17 = (bf16[4,96,768]{2,1,0:T(8,128)(2,1)S(1)}, bf16[4,96,768]{2,1,0:T(8,128)(2,1)}, u32[]{:S(2)}, u32[]{:S(2)}) collective-permute-start(bf16[4,96,768]{2,1,0:T(8,128)(2,1)S(1)} %collective-permute-done.15.rest_1_), channel_id=1, source_target_pairs={{0,16},{16,0},{1,17},{17,1},{2,18},{18,2},{3,19},{19,3},{4,20},{20... | collective-permute-start | bytes 1769480 | tf_op jit(solution)/shard_map/ppermute | solution.py:896
  151.1 51.2 %collective-permute-start.20 = (bf16[4,96,768]{2,1,0:T(8,128)(2,1)S(1)}, bf16[4,96,768]{2,1,0:T(8,128)(2,1)S(1)}, u32[]{:S(2)}, u32[]{:S(2)}) collective-permute-start(bf16[4,96,768]{2,1,0:T(8,128)(2,1)S(1)} %collective-permute-done.16.rest_2_), channel_id=1, source_target_pairs={{0,1},{1,0},{2,3},{3,2},{4,5},{5,4},{6,7},{7,6},{8,9},{9,8},{10,11... | collective-permute-start | bytes 1769480 | tf_op jit(solution)/shard_map/ppermute | solution.py:896
  151.1 52.5 %collective-permute-start.27 = (bf16[4,192,384]{2,1,0:T(8,128)(2,1)}, bf16[4,192,384]{2,1,0:T(8,128)(2,1)}, u32[]{:S(2)}, u32[]{:S(2)}) collective-permute-start(bf16[4,192,384]{2,1,0:T(8,128)(2,1)} %collective-permute-done.26.rest_10_), channel_id=1, source_target_pairs={{0,2},{2,0},{1,3},{3,1},{4,6},{6,4},{5,7},{7,5},{8,10},{10,8},{9,1... | collective-permute-start | bytes 1769480 | tf_op jit(solution)/shard_map/ppermute | solution.py:896
  262.9 41.0 %collective-permute-start.54 = (bf16[2,2,4,96,256]{4,3,2,1,0:T(8,128)(2,1)}, bf16[2,2,4,96,256]{4,3,2,1,0:T(8,128)(2,1)S(1)}, u32[]{:S(2)}, u32[]{:S(2)}) collective-permute-start(bf16[2,2,4,96,256]{4,3,2,1,0:T(8,128)(2,1)} %get-tuple-element.59), channel_id=1, source_target_pairs={{0,1},{1,0},{2,3},{3,2},{4,5},{5,4},{6,7},{7,6},{8,9},{9,8},{10,11... | collective-permute-start | bytes 2359304 | tf_op jit(solution)/shard_map/ppermute | solution.py:896
  263.1 147.9 %collective-permute-start.42 = (bf16[512,768]{1,0:T(8,128)(2,1)}, bf16[512,768]{1,0:T(8,128)(2,1)}, u32[]{:S(2)}, u32[]{:S(2)}) collective-permute-start(bf16[512,768]{1,0:T(8,128)(2,1)} %get-tuple-element.123), channel_id=1, source_target_pairs={{0,0},{4,1},{2,2},{6,3},{8,4},{12,5},{10,6},{14,7},{1,8},{5,9},{3,... | collective-permute-start | bytes 2359304 | tf_op jit(solution)/shard_map/ppermute | solution.py:976
  270.5 142.1 %collective-permute-start.43 = (bf16[512,768]{1,0:T(8,128)(2,1)}, bf16[512,768]{1,0:T(8,128)(2,1)}, u32[]{:S(2)}, u32[]{:S(2)}) collective-permute-start(bf16[512,768]{1,0:T(8,128)(2,1)} %get-tuple-element.124), channel_id=1, source_target_pairs={{8,0},{12,1},{10,2},{14,3},{0,4},{4,5},{2,6},{6,7},{9,8},{13,9},{1... | collective-permute-start | bytes 2359304 | tf_op jit(solution)/shard_map/ppermute | solution.py:977
  270.5 33.8 %collective-permute-start.44 = (bf16[1024,384]{1,0:T(8,128)(2,1)}, bf16[1024,384]{1,0:T(8,128)(2,1)S(1)}, u32[]{:S(2)}, u32[]{:S(2)}) collective-permute-start(bf16[1024,384]{1,0:T(8,128)(2,1)} %get-tuple-element.48), channel_id=1, source_target_pairs={{0,1},{1,0},{2,3},{3,2},{4,5},{5,4},{6,7},{7,6},{8,9},{9,8},{10,11... | collective-permute-start | bytes 2359304 | tf_op jit(solution)/shard_map/ppermute | solution.py:896
  290.6 156.5 %collective-permute-start.60 = (bf16[2,2,4,96,768]{4,3,2,1,0:T(8,128)(2,1)}, bf16[2,2,4,96,768]{4,3,2,1,0:T(8,128)(2,1)}, u32[]{:S(2)}, u32[]{:S(2)}) collective-permute-start(bf16[2,2,4,96,768]{4,3,2,1,0:T(8,128)(2,1)} %bitcast.231), channel_id=1, source_target_pairs={{0,1},{1,0},{2,3},{3,2},{4,5},{5,4},{6,7},{7,6},{8,9},{9,8},{10,11... | collective-permute-start | bytes 7077896 | tf_op jit(solution)/shard_map/ppermute | solution.py:896
  304.0 148.1 %collective-permute-start.66 = (bf16[2,2,4,192,384]{4,3,2,1,0:T(8,128)(2,1)}, bf16[2,2,4,192,384]{4,3,2,1,0:T(8,128)(2,1)}, u32[]{:S(2)}, u32[]{:S(2)}) collective-permute-start(bf16[2,2,4,192,384]{4,3,2,1,0:T(8,128)(2,1)} %get-tuple-element.65), channel_id=1, source_target_pairs={{0,1},{1,0},{2,3},{3,2},{4,5},{5,4},{6,7},{7,6},{8,9},{9,8},{10,11... | collective-permute-start | bytes 7077896 | tf_op jit(solution)/shard_map/ppermute | solution.py:896
  304.3 117.6 %collective-permute-start.55 = (bf16[2,4,96,256]{3,2,1,0:T(8,128)(2,1)S(1)}, bf16[2,4,96,256]{3,2,1,0:T(8,128)(2,1)}, u32[]{:S(2)}, u32[]{:S(2)}) collective-permute-start(bf16[2,4,96,256]{3,2,1,0:T(8,128)(2,1)S(1)} %get-tuple-element.116), channel_id=1, source_target_pairs={{0,16},{16,0},{1,17},{17,1},{2,18},{18,2},{3,19},{19,3},{4,20},{20... | collective-permute-start | bytes 1179656 | tf_op jit(solution)/shard_map/ppermute | solution.py:896
  411.0 34.5 %collective-permute-start.48 = (bf16[2,4,3,96,256]{4,3,2,1,0:T(8,128)(2,1)S(1)}, bf16[2,4,3,96,256]{4,3,2,1,0:T(8,128)(2,1)S(1)}, u32[]{:S(2)}, u32[]{:S(2)}) collective-permute-start(bf16[2,4,3,96,256]{4,3,2,1,0:T(8,128)(2,1)S(1)} %copy-done.25), channel_id=1, source_target_pairs={{0,2},{2,0},{1,3},{3,1},{4,6},{6,4},{5,7},{7,5},{8,10},{10,8},{9,1... | collective-permute-start | bytes 3538952 | tf_op jit(solution)/shard_map/ppermute | solution.py:896
  412.6 43.7 %collective-permute-start.45 = (bf16[1024,768]{1,0:T(8,128)(2,1)}, bf16[1024,768]{1,0:T(8,128)(2,1)S(1)}, u32[]{:S(2)}, u32[]{:S(2)}) collective-permute-start(bf16[1024,768]{1,0:T(8,128)(2,1)} %grad_token.3), channel_id=1, source_target_pairs={{0,1},{1,0},{2,3},{3,2},{4,5},{5,4},{6,7},{7,6},{8,9},{9,8},{10,11... | collective-permute-start | bytes 4718600 | tf_op jit(solution)/shard_map/ppermute | solution.py:896
  450.5 39.2 %collective-permute-start.61 = (bf16[2,4,96,768]{3,2,1,0:T(8,128)(2,1)}, bf16[2,4,96,768]{3,2,1,0:T(8,128)(2,1)}, u32[]{:S(2)}, u32[]{:S(2)}) collective-permute-start(bf16[2,4,96,768]{3,2,1,0:T(8,128)(2,1)} %get-tuple-element.112), channel_id=1, source_target_pairs={{0,2},{2,0},{1,3},{3,1},{4,6},{6,4},{5,7},{7,5},{8,10},{10,8},{9,1... | collective-permute-start | bytes 3538952 | tf_op jit(solution)/shard_map/ppermute | solution.py:896
  455.6 36.7 %collective-permute-start.67 = (bf16[2,4,192,384]{3,2,1,0:T(8,128)(2,1)}, bf16[2,4,192,384]{3,2,1,0:T(8,128)(2,1)}, u32[]{:S(2)}, u32[]{:S(2)}) collective-permute-start(bf16[2,4,192,384]{3,2,1,0:T(8,128)(2,1)} %get-tuple-element.101), channel_id=1, source_target_pairs={{0,16},{16,0},{1,17},{17,1},{2,18},{18,2},{3,19},{19,3},{4,20},{20... | collective-permute-start | bytes 3538952 | tf_op jit(solution)/shard_map/ppermute | solution.py:896
  486.1 32.2 %collective-permute-start.47 = (bf16[512,768]{1,0:T(8,128)(2,1)}, bf16[512,768]{1,0:T(8,128)(2,1)}, u32[]{:S(2)}, u32[]{:S(2)}) collective-permute-start(bf16[512,768]{1,0:T(8,128)(2,1)} %get-tuple-element.120), channel_id=1, source_target_pairs={{8,0},{12,1},{10,2},{14,3},{0,4},{4,5},{2,6},{6,7},{9,8},{13,9},{1... | collective-permute-start | bytes 2359304 | tf_op jit(solution)/shard_map/ppermute | solution.py:977
  491.0 30.7 %collective-permute-start.62 = (bf16[4,96,768]{2,1,0:T(8,128)(2,1)S(1)}, bf16[4,96,768]{2,1,0:T(8,128)(2,1)S(1)}, u32[]{:S(2)}, u32[]{:S(2)}) collective-permute-start(bf16[4,96,768]{2,1,0:T(8,128)(2,1)S(1)} %fusion.5), channel_id=1, source_target_pairs={{0,16},{16,0},{1,17},{17,1},{2,18},{18,2},{3,19},{19,3},{4,20},{20... | collective-permute-start | bytes 1769480 | tf_op jit(solution)/shard_map/ppermute | solution.py:896
  493.5 33.0 %collective-permute-start.68 = (bf16[4,192,384]{2,1,0:T(8,128)(2,1)S(1)}, bf16[4,192,384]{2,1,0:T(8,128)(2,1)S(1)}, u32[]{:S(2)}, u32[]{:S(2)}) collective-permute-start(bf16[4,192,384]{2,1,0:T(8,128)(2,1)S(1)} %fusion.6), channel_id=1, source_target_pairs={{0,2},{2,0},{1,3},{3,1},{4,6},{6,4},{5,7},{7,5},{8,10},{10,8},{9,1... | collective-permute-start | bytes 1769480 | tf_op jit(solution)/shard_map/ppermute | solution.py:896
  (75 other events, 948.2 us)
